TPU v7x, 256 devices: a whole 4x4x8 slice. The times are simulated.
256 devices in a mesh: dp: 32 (over z, y), tensor: 8 (over x, core).
Axes of the slice: x: 4, y: 4, z: 8, core: 2. Of those that a mesh axis runs over, the one named last changes fastest.
Arguments:
- context: bfloat16 [65536, 8192], P('dp', 'tensor'), may hold values from -0.3125 to 0.3125
- out_grad: bfloat16 [65536, 1024], P(('dp', 'tensor')), may hold values from -6 to 6
- out_weight: bfloat16 [8192, 1024], P('tensor'), may hold values from -0.1875 to 0.1875
- error: bfloat16 [32, 8192, 1024], P('dp', 'tensor'), may hold values from -23 to 23
- q_init: float32 [1024, 64], replicated, may hold values from -6 to 6
Outputs:
- ctx_grad: bfloat16 [65536, 8192], P('dp', 'tensor')
- new_error: bfloat16 [32, 8192, 1024], P('dp', 'tensor')
- q_factor: float32 [1024, 64], replicated
All inputs are finite; a program needn't handle non-finite values.
Results may differ from a plain program's by a relative error of at most 0.0085.
Values may be sent and summed in bfloat16 or wider, within the bound.
A program may use at most 64 MiB of HBM per device.

v0:
```python
import jax
import jax.numpy as jnp
from jax import lax
from jax.sharding import PartitionSpec as P

HIGH = lax.Precision.HIGHEST


def shards(context, out_grad, out_weight, error, q_init):
    replicas = lax.axis_size("dp")
    piece = lax.all_gather(out_grad, "tensor", axis=0, tiled=True)
    grad_total = lax.dot_general(
        context, piece, (((0,), (0,)), ((), ())), preferred_element_type=jnp.float32
    )
    rows_out = lax.dot_general(
        piece, out_weight, (((1,), (1,)), ((), ())), preferred_element_type=jnp.float32
    )
    ctx_total = rows_out.astype(jnp.bfloat16)
    grad_total, ctx_grad = (grad_total, ctx_total)
    grad = grad_total.astype(jnp.bfloat16)
    merged = grad.astype(jnp.float32) + error[0].astype(jnp.float32)
    p_part = jnp.dot(merged, q_init, precision=HIGH)
    p_mean = lax.psum(p_part.astype(jnp.bfloat16), "dp").astype(jnp.float32) / replicas
    gram = lax.psum(jnp.dot(p_mean.T, p_mean, precision=HIGH), "tensor")
    chol = jnp.linalg.cholesky(gram)
    p_factor = jax.scipy.linalg.solve_triangular(chol, p_mean.T, lower=True).T
    q_part = lax.dot_general(merged, p_factor, (((0,), (0,)), ((), ())), precision=HIGH)
    q_factor = lax.psum(q_part, ("dp", "tensor")) / replicas
    new_error = (merged - jnp.dot(p_factor, q_factor.T, precision=HIGH)).astype(jnp.bfloat16)
    return (ctx_grad, new_error[None], q_factor)


def solution(mesh):
    placed = (
        P("dp", "tensor"),
        P(("dp", "tensor"), None),
        P("tensor", None),
        P("dp", "tensor", None),
        P(),
    )
    return jax.shard_map(
        shards,
        mesh=mesh,
        in_specs=placed,
        out_specs=(P("dp", "tensor"), P("dp", "tensor", None), P()),
        check_vma=False,
    )
```

profile of v0, /device:TPU:1, one launch (start us, length us, event | category | flops | bytes accessed | tf_op | source)
XLA Modules:
  0.0 507.6 jit_solution(3773945723848760019)
XLA Ops:
  7.2 0.0 copy-start
  7.2 0.0 all-gather.2.cloned.1.call-start
  7.2 0.7 all-gather.2.cloned.1.call-update
  7.9 0.0 copy-start.4
  7.9 0.0 all-reduce.3.cloned.1.call-start
  8.0 40.8 %all-gather.2.cloned.1.call-done = bf16[2048,1024]{1,0:T(8,128)(2,1)} async-done(((bf16[256,1024]{1,0:T(8,128)(2,1)}), bf16[2048,1024]{1,0:T(8,128)(2,1)}) %all-gather.2.cloned.1.call-update) | async-done | bytes 4194320 | tf_op jit(solution)/shard_map/all_gather | solution.py:11
  48.8 8.2 %convolution_convert_fusion.1 = bf16[1024,1024]{1,0:T(8,128)(2,1)S(1)} fusion(bf16[2048,1024]{1,0:T(8,128)(2,1)} %param.5, bf16[2048,1024]{1,0:T(8,128)(2,1)} %all-gather.2.cloned.1.call-done), kind=kOutput, calls=%fused_computation.7 | convolution fusion | flops 4296015872 | bytes 10485760 | tf_op jit(solution)/shard_map/dot_general | solution.py:12
  57.0 0.0 copy-start.2
  57.0 1.3 copy-done.2
  58.3 0.0 copy-done.4
  58.3 0.0 copy-done.1
  58.3 5.2 %fusion.5 = bf16[1024,64]{0,1:T(8,128)(2,1)} fusion(f32[1024,64]{0,1:T(8,128)S(1)} %copy-done.4, bf16[1024,1024]{1,0:T(8,128)(2,1)S(1)} %convolution_convert_fusion.1, bf16[1,1024,1024]{2,1,0:T(8,128)(2,1)S(1)} %copy-done.1), kind=kOutput, calls=%fused_computation.9 | convolution fusion | flops 808517632 | bytes 4587520 | tf_op jit(solution)/shard_map/dot_general | solution.py:22
  63.5 0.0 all-reduce.3.cloned.1.call-update
  63.5 0.0 all-reduce.5.cloned.1.call-start
  63.5 136.7 %all-reduce.3.cloned.1.call-done = bf16[1024,64]{0,1:T(8,128)(2,1)} async-done(((bf16[1024,64]{0,1:T(8,128)(2,1)}), bf16[1024,64]{0,1:T(8,128)(2,1)}) %all-reduce.3.cloned.1.call-update) | async-done | bytes 131088 | tf_op jit(solution)/shard_map/psum | solution.py:23
  200.2 1.4 fusion.7
  201.6 24.7 %psum.22 = f32[64,64]{0,1:T(8,128)S(1)} all-reduce(f32[64,64]{0,1:T(8,128)S(1)} %fusion.7), channel_id=1, replica_groups=mesh['dp'=32,'tensor'=8] {'tensor'}, use_global_device_ids=true, to_apply=%region_1.0 | all-reduce | flops 4096 | bytes 32768 | tf_op jit(solution)/shard_map/psum | solution.py:24
  226.2 0.1 copy.9
  226.3 5.8 %cholesky.16 = f32[64,64]{1,0:T(8,128)S(1)} custom-call(f32[64,64]{1,0:T(8,128)S(1)} %fusion.12), custom_call_target="Cholesky" | custom-call | tf_op jit(solution)/shard_map/jit(cholesky)/cholesky | solution.py:25
  232.2 0.6 compare_reduce_fusion
  232.8 0.7 fusion.10
  233.5 4.9 custom-call.7
  238.4 1.3 fusion.6
  239.7 6.1 %fusion = f32[1024,64]{0,1:T(8,128)} fusion(f32[64,1024]{1,0:T(8,128)S(1)} %fusion.6, bf16[1024,1024]{1,0:T(8,128)(2,1)} %copy-done.2, bf16[1,1024,1024]{2,1,0:T(8,128)(2,1)} %param.8), kind=kOutput, calls=%fused_computation.3 | convolution fusion | flops 808452096 | bytes 4718592 | tf_op jit(solution)/shard_map/dot_general | solution.py:27
  245.8 0.0 all-reduce.5.cloned.1.call-update
  245.8 0.0 copy-done
  245.8 8.3 %convolution_convert_fusion = bf16[2048,1024]{1,0:T(8,128)(2,1)} fusion(bf16[2048,1024]{1,0:T(8,128)(2,1)} %all-gather.2.cloned.1.call-done, bf16[1024,1024]{1,0:T(8,128)(2,1)S(1)} %copy-done), kind=kOutput, calls=%fused_computation.2 | convolution fusion | flops 4297064448 | bytes 10485760 | tf_op jit(solution)/shard_map/dot_general | solution.py:15
  254.2 239.4 %all-reduce.5.cloned.1.call-done = f32[1024,64]{0,1:T(8,128)} async-done(((f32[1024,64]{0,1:T(8,128)}), f32[1024,64]{0,1:T(8,128)}) %all-reduce.5.cloned.1.call-update) | async-done | bytes 262160 | tf_op jit(solution)/shard_map/psum | solution.py:28
  493.6 1.0 broadcast_multiply_fusion
  494.5 0.0 copy-start.3
  494.5 6.6 %fusion.4 = bf16[1,1024,1024]{2,1,0:T(8,128)(2,1)} fusion(f32[64,1024]{1,0:T(8,128)S(1)} %fusion.6, f32[1024,64]{0,1:T(8,128)S(1)} %broadcast_multiply_fusion, bf16[1,1024,1024]{2,1,0:T(8,128)(2,1)} %param.8, bf16[1024,1024]{1,0:T(8,128)(2,1)} %copy-done.2), kind=kOutput, calls=%fused_computation.8 | convolution fusion | flops 810549248 | bytes 6815744 | tf_op jit(solution)/shard_map/dot_general | solution.py:29
  501.1 0.0 copy-done.3
  (3 shorter events, 0.0 us)
Async XLA Ops:
  7.2 238.7 %copy-start = (bf16[1024,1024]{1,0:T(8,128)(2,1)S(1)}, bf16[1024,1024]{1,0:T(8,128)(2,1)}, u32[]{:S(2)}) copy-start(bf16[1024,1024]{1,0:T(8,128)(2,1)} %param.7) | copy-start | bytes 6291460
  7.2 41.6 %all-gather.2.cloned.1.call-start = ((), (), s32[]{:S(2)}) async-start(), calls=%async_computation | async-start | bytes 4718592 | tf_op jit(solution)/shard_map/all_gather | solution.py:11
  7.9 50.4 %copy-start.4 = (f32[1024,64]{0,1:T(8,128)S(1)}, f32[1024,64]{0,1:T(8,128)}, u32[]{:S(2)}) copy-start(f32[1024,64]{0,1:T(8,128)} %param.9) | copy-start | bytes 786436
  7.9 192.3 %all-reduce.3.cloned.1.call-start = ((), (), s32[]{:S(2)}) async-start(), calls=%async_computation.1 | async-start | bytes 262144 | tf_op jit(solution)/shard_map/psum | solution.py:23
  48.8 9.5 %copy-start.1 = (bf16[1,1024,1024]{2,1,0:T(8,128)(2,1)S(1)}, bf16[1,1024,1024]{2,1,0:T(8,128)(2,1)}, u32[]{:S(2)}) copy-start(bf16[1,1024,1024]{2,1,0:T(8,128)(2,1)} %param.8) | copy-start | bytes 6291460
  57.0 1.3 copy-start.2
  63.5 430.1 %all-reduce.5.cloned.1.call-start = ((), (), s32[]{:S(2)}) async-start(), calls=%async_computation.2 | async-start | bytes 524288 | tf_op jit(solution)/shard_map/psum | solution.py:28
  494.5 6.6 %copy-start.3 = (f32[1024,64]{0,1:T(8,128)}, f32[1024,64]{0,1:T(8,128)S(1)}, u32[]{:S(2)}) copy-start(f32[1024,64]{0,1:T(8,128)S(1)} %broadcast_multiply_fusion) | copy-start | bytes 786436
Sparse Core Ops, SparseCore 0:
  9.9 38.8 all-gather.1
  63.6 136.5 all-reduce.2
  246.0 247.5 all-reduce.4
where the time goes:
time: 508 us
  waiting for transfers between devices  418 us (82%)
  matrix products  37 us (7%)
  blocking collectives  24.7 us (5%)
  between operations  13.8 us (3%)
  other arithmetic  13 us (3%)
    psum x1, waiting for transfers between devices, shards(): q_factor = lax.psum(q_part, ('dp', 'tensor')) / replicas  239 us
    psum x1, waiting for transfers between devices, shards(): lax.psum(p_part.astype(jnp.bfloat16), 'dp').astype(jnp.float32) / replicas  137 us
    all_gather x1, waiting for transfers between devices, shards(): piece = lax.all_gather(out_grad, 'tensor', axis=0, tiled=True)  40.8 us
    psum x1, blocking collectives, shards(): gram = lax.psum(jnp.dot(p_mean.T, p_mean, precision=HIGH), 'tensor')  24.7 us
  transfers between devices with their start and end apart: 3, of which 3 were waited for; matrix products, arithmetic and copies ran while one was open for 2% of the time, Pallas kernels for 0%

commit v1 on v0

v1 whole, which is shorter than its diff:
```python
import functools

import jax
import jax.numpy as jnp
from jax import lax
from jax.experimental import pallas as pl
from jax.experimental.pallas import tpu as pltpu
from jax.sharding import PartitionSpec as P

MESH = pl.DeviceIdType.MESH
F32 = jnp.float32
BF16 = jnp.bfloat16
NX = 4
RANK = 64
BLOCKS = 4
NT = (((1,), (1,)), ((), ()))
NN = (((1,), (0,)), ((), ()))


def dot(a, b, dims=NN):
    return lax.dot_general(a, b, dims, preferred_element_type=F32)


def split(v):
    hi = v.astype(BF16)
    return hi, (v - hi.astype(F32)).astype(BF16)


def eliminate(a, first, last):
    row_ids = lax.broadcasted_iota(jnp.int32, a.shape, 0)
    for k in range(first, last):
        col = jnp.broadcast_to(a[:, k : k + 1], a.shape)
        row = a[k : k + 1, :] / col[k : k + 1, :]
        a = a - jnp.where(row_ids > k, col, 0.0) * row
    return a


def kernel(
    ny, nz,
    ctx_hbm, dy_hbm, w_hbm, e_hbm, q_hbm,
    dctx_hbm, ne_hbm, qf_hbm,
    cv, ct, og, wv, ev, qv, q2, yg, pe, gb, ps, prx, pall, pt,
    gx1, gx2, aug, ze, zs, z1, z2, zall, ft, qs, cs, ns, qo,
    load, store, y_send, y_near, y_sib, o_send, o_left, o_right, o_far, o_sib,
    p_send, p_recv, g_send, g_recv, z_send, z_recv,
):
    dp, ten = lax.axis_index("dp"), lax.axis_index("tensor")
    z, y = dp // ny, dp % ny
    x, core = ten // 2, ten % 2
    ndp, nten = ny * nz, 2 * NX
    nplane = ny * nten
    rows = dy_hbm.shape[0]
    half = rows // 2
    tokens = rows * nten
    width = og.shape[2]
    inner, d = w_hbm.shape
    xl, xr, xo = lax.rem(x + NX - 1, NX), lax.rem(x + 1, NX), lax.rem(x + 2, NX)
    sib = {"tensor": 2 * x + 1 - core}
    left, right, far = ({"tensor": 2 * i + core} for i in (xl, xr, xo))

    barrier = pltpu.get_barrier_semaphore()

    @pl.loop(1, nten)
    def _(j):
        pl.semaphore_signal(barrier, inc=1, device_id={"tensor": lax.rem(ten + j, nten)}, device_id_type=MESH)

    @pl.loop(1, ndp)
    def _(j):
        pl.semaphore_signal(barrier, inc=1, device_id={"dp": lax.rem(dp + j, ndp)}, device_id_type=MESH)

    def piece(b, owner, part=None):
        if part is None:
            return og.at[b, pl.ds(pl.multiple_of(owner * rows, rows), rows)]
        return og.at[b, pl.ds(pl.multiple_of(owner * rows + part * half, half), half)]

    def send(src, dst, s_sem, r_sem, dev):
        pltpu.make_async_remote_copy(
            src_ref=src, dst_ref=dst, send_sem=s_sem, recv_sem=r_sem, device_id=dev, device_id_type=MESH
        ).start()

    def await_bytes(ref, sem):
        pltpu.make_async_copy(ref, ref, sem).wait()

    loads = []
    for b in range(BLOCKS):
        loads.append(pltpu.make_async_copy(dy_hbm.at[:, pl.ds(b * width, width)], piece(b, ten), load.at[b]))
    load_q = pltpu.make_async_copy(q_hbm, qv, load.at[BLOCKS])
    load_e = pltpu.make_async_copy(e_hbm.at[0], ev, load.at[BLOCKS + 1])
    load_c = pltpu.make_async_copy(ctx_hbm, cv, load.at[BLOCKS + 2])
    load_w = pltpu.make_async_copy(w_hbm, wv, load.at[BLOCKS + 3])
    for c in [load_q, *loads, load_e, load_c, load_w]:
        c.start()

    load_q.wait()
    hi, lo = split(qv[...].T)
    q2[0:RANK] = hi
    q2[RANK : 2 * RANK] = lo
    for c in loads:
        c.wait()
    yv = jnp.zeros((2 * RANK, rows), F32)
    own = pl.ds(pl.multiple_of(ten * rows, rows), rows)
    for b in range(BLOCKS):
        yv += dot(q2[:, b * width : (b + 1) * width], og[b, own, :], NT)
    yg[ten] = (yv[:RANK] + yv[RANK:]).astype(BF16)

    pl.semaphore_wait(barrier, nten - 1 + ndp - 1)

    for dev in (right, left, far):
        send(yg.at[ten], yg.at[ten], y_send, y_near, dev)
    send(yg.at[ten], yg.at[ten], y_send, y_sib, sib)

    def send_own(b):
        mine = piece(b, ten)
        send(mine, mine, o_send.at[b], o_left.at[b], right)
        send(mine, mine, o_send.at[b], o_right.at[b], left)
        send(mine, mine, o_send.at[b], o_sib.at[b], sib)

    def pass_near(b):
        from_left, from_right = piece(b, 2 * xl + core), piece(b, 2 * xr + core)
        await_bytes(from_left, o_left.at[b])
        onward = piece(b, 2 * xl + core, 0)
        send(onward, onward, o_send.at[b], o_far.at[b], right)
        send(from_left, from_left, o_send.at[b], o_sib.at[b], sib)
        await_bytes(from_right, o_right.at[b])
        onward = piece(b, 2 * xr + core, 1)
        send(onward, onward, o_send.at[b], o_far.at[b], left)
        send(from_right, from_right, o_send.at[b], o_sib.at[b], sib)

    def pass_far(b):
        from_far = piece(b, 2 * xo + core)
        await_bytes(from_far, o_far.at[b])
        send(from_far, from_far, o_send.at[b], o_sib.at[b], sib)

    def grad_block(b):
        await_bytes(og.at[b, pl.ds(0, rows * NX)], o_sib.at[b])
        mt = min(512, inner)

        @pl.loop(0, inner // mt)
        def _(i):
            r = pl.ds(pl.multiple_of(i * mt, mt), mt)
            gb[r, b * width : (b + 1) * width] = dot(ct[r, :], og[b]).astype(BF16)

    send_own(0)
    send_own(1)

    load_e.wait()
    for n in range(4):
        r = slice(n * inner // 4, (n + 1) * inner // 4)
        v = dot(q2[...], ev[r, :], NT)
        pe[:, r] = v[:RANK] + v[RANK:]
    load_c.wait()
    for t in range(nten):
        ct[:, t * rows : (t + 1) * rows] = cv[t * rows : (t + 1) * rows, :].T

    await_bytes(yg.at[pl.ds(0, 3)], y_near)
    for i in (xl, xr, xo):
        got = yg.at[2 * i + core]
        send(got, got, y_send, y_sib, sib)
    await_bytes(yg.at[pl.ds(0, 4)], y_sib)

    pv = pe[...]
    for t in range(nten):
        pv += dot(yg[t], cv[t * rows : (t + 1) * rows, :])
    pr, pc = RANK // ny, inner // nz
    pv = pv.astype(BF16)
    for k in range(ndp):
        ps[k] = pv[(k % ny) * pr : (k % ny + 1) * pr, (k // ny) * pc : (k // ny + 1) * pc]

    @pl.loop(1, ndp)
    def _(j):
        to = lax.rem(dp + j, ndp)
        send(ps.at[to], prx.at[dp], p_send.at[0], p_recv.at[0], {"dp": to})

    prx[dp] = ps[dp]
    pass_near(0)
    send_own(2)

    await_bytes(prx.at[pl.ds(0, ndp - 1)], p_recv.at[0])
    total = prx[0].astype(F32)
    for k in range(1, ndp):
        total += prx[k].astype(F32)
    pall[dp] = (total * (1.0 / ndp)).astype(BF16)

    @pl.loop(1, ndp)
    def _(j):
        send(pall.at[dp], pall.at[dp], p_send.at[1], p_recv.at[1], {"dp": lax.rem(dp + j, ndp)})

    pass_near(1)
    send_own(3)
    pass_far(0)
    grad_block(0)

    await_bytes(pall.at[pl.ds(0, ndp - 1)], p_recv.at[1])
    for k in range(ndp):
        pt[(k % ny) * pr : (k % ny + 1) * pr, (k // ny) * pc : (k // ny + 1) * pc] = pall[k]
    gram = dot(pt[...], pt[...], NT)
    gx1[core] = jnp.concatenate([gram[: RANK // 2], gram[RANK // 2 :]], axis=1)
    send(gx1.at[core], gx1.at[core], g_send.at[0], g_recv.at[0], sib)
    pass_far(1)
    pass_near(2)
    ze[...] = dot(pt[...], ev[...])
    await_bytes(gx1.at[0], g_recv.at[0])
    gx2[x] = gx1[0] + gx1[1]
    for dev in (right, left, far):
        send(gx2.at[x], gx2.at[x], g_send.at[1], g_recv.at[1], dev)
    grad_block(1)
    pass_near(3)
    pass_far(2)

    await_bytes(gx2.at[pl.ds(0, NX - 1)], g_recv.at[1])
    gram = gx2[0] + gx2[1] + gx2[2] + gx2[3]
    gram = jnp.concatenate([gram[:, :RANK], gram[:, RANK:]], axis=0)
    eye = (
        lax.broadcasted_iota(jnp.int32, (RANK, RANK), 0) == lax.broadcasted_iota(jnp.int32, (RANK, RANK), 1)
    ).astype(F32)
    aug[...] = eliminate(jnp.concatenate([gram, eye], axis=1), 0, 24)
    grad_block(2)
    pass_far(3)
    grad_block(3)

    zv = ze[...] + dot(pt[...], gb[...])
    zr, zc = RANK // ny, d // nten
    for k in range(nplane):
        zs[k] = zv[(k % ny) * zr : (k % ny + 1) * zr, (k // ny) * zc : (k // ny + 1) * zc]
    me = ten * ny + y

    @pl.loop(1, nplane)
    def _(j):
        to = lax.rem(me + j, nplane)
        send(zs.at[to], z1.at[me], z_send.at[0], z_recv.at[0], {"dp": z * ny + to % ny, "tensor": to // ny})

    z1[me] = zs[me]

    load_w.wait()
    out_rows = tokens // 4

    def ctx_chunk(i):
        r = pl.ds(i * out_rows, out_rows)
        for n in range(4):
            c = slice(n * inner // 4, (n + 1) * inner // 4)
            acc = dot(og[0, r, :], wv[c, 0:width], NT)
            for b in range(1, BLOCKS):
                acc += dot(og[b, r, :], wv[c, b * width : (b + 1) * width], NT)
            cs[r, c] = acc.astype(BF16)
        out = pltpu.make_async_copy(cs.at[r], dctx_hbm.at[r], store.at[i])
        out.start()
        return out

    outs = [ctx_chunk(0), ctx_chunk(1)]

    await_bytes(z1.at[pl.ds(0, nplane - 1)], z_recv.at[0])
    total = z1[0]
    for k in range(1, nplane):
        total += z1[k]
    z2[z] = total

    @pl.loop(1, nz)
    def _(j):
        to = lax.rem(z + j, nz)
        send(z2.at[z], z2.at[z], z_send.at[1], z_recv.at[1], {"dp": to * ny + y})

    a = eliminate(aug[...], 24, RANK)
    on_diag = lax.broadcasted_iota(jnp.int32, (RANK, RANK), 0) == lax.broadcasted_iota(jnp.int32, (RANK, RANK), 1)
    diag = jnp.sum(jnp.where(on_diag, a[:, :RANK], 0.0), axis=1, keepdims=True)
    inv = a[:, RANK:] / jnp.sqrt(diag)
    inv_hi, inv_lo = split(inv)
    f = dot(inv_hi, pt[...]) + dot(inv_lo, pt[...])
    f_hi, f_lo = split(f)
    ft[...] = jnp.concatenate([f_hi, f_lo, f_hi], axis=0).T

    await_bytes(z2.at[pl.ds(0, nz - 1)], z_recv.at[1])
    total = z2[0]
    for k in range(1, nz):
        total += z2[k]
    zall[me] = total * (1.0 / ndp)

    @pl.loop(1, nplane)
    def _(j):
        to = lax.rem(me + j, nplane)
        send(zall.at[me], zall.at[me], z_send.at[2], z_recv.at[2], {"dp": z * ny + to % ny, "tensor": to // ny})

    outs += [ctx_chunk(2), ctx_chunk(3)]

    await_bytes(zall.at[pl.ds(0, nplane - 1)], z_recv.at[2])
    for k in range(nplane):
        hi, lo = split(zall[k])
        r, c = (k % ny) * zr, slice((k // ny) * zc, (k // ny + 1) * zc)
        qs[r : r + zr, c] = hi
        qs[RANK + r : RANK + r + zr, c] = hi
        qs[2 * RANK + r : 2 * RANK + r + zr, c] = lo
    qt = dot(jnp.concatenate([inv_hi, inv_lo, inv_hi], axis=1), qs[...])
    qo[...] = qt.T
    out = pltpu.make_async_copy(qo, qf_hbm, store.at[4])
    out.start()
    outs.append(out)
    hi, lo = split(qt)
    qs[0:RANK] = hi
    qs[RANK : 2 * RANK] = hi
    qs[2 * RANK : 3 * RANK] = lo
    ne_rows = inner // 4
    for i in range(4):
        r = pl.ds(i * ne_rows, ne_rows)
        low = dot(ft[r, :], qs[...])
        ns[r, :] = (gb[r, :].astype(F32) + ev[r, :].astype(F32) - low).astype(BF16)
        out = pltpu.make_async_copy(ns.at[r], ne_hbm.at[0, r], store.at[5 + i])
        out.start()
        outs.append(out)

    await_bytes(yg.at[pl.ds(0, 7)], y_send)
    for b in range(BLOCKS):
        await_bytes(og.at[b, pl.ds(0, 7 * rows)], o_send.at[b])
    await_bytes(prx.at[pl.ds(0, ndp - 1)], p_send.at[0])
    await_bytes(pall.at[pl.ds(0, ndp - 1)], p_send.at[1])
    await_bytes(gx1.at[0], g_send.at[0])
    await_bytes(gx2.at[pl.ds(0, NX - 1)], g_send.at[1])
    await_bytes(z1.at[pl.ds(0, nplane - 1)], z_send.at[0])
    await_bytes(z2.at[pl.ds(0, nz - 1)], z_send.at[1])
    await_bytes(zall.at[pl.ds(0, nplane - 1)], z_send.at[2])
    for out in outs:
        out.wait()


def shards(ny, nz, context, out_grad, out_weight, error, q_init):
    tokens, inner = context.shape
    rows, d = out_grad.shape
    ndp, nplane = ny * nz, 2 * NX * ny
    width = d // BLOCKS
    dma = pltpu.SemaphoreType.DMA
    any_ = pl.BlockSpec(memory_space=pl.ANY)
    pr, pc = RANK // ny, inner // nz
    zr, zc = RANK // ny, d // (2 * NX)
    vm = pltpu.VMEM
    return pl.pallas_call(
        functools.partial(kernel, ny, nz),
        out_shape=(
            jax.ShapeDtypeStruct((tokens, inner), BF16),
            jax.ShapeDtypeStruct((1, inner, d), BF16),
            jax.ShapeDtypeStruct((d, RANK), F32),
        ),
        in_specs=[any_] * 5,
        out_specs=(any_, any_, any_),
        scratch_shapes=[
            vm((tokens, inner), BF16),
            vm((inner, tokens), BF16),
            vm((BLOCKS, tokens, width), BF16),
            vm((inner, d), BF16),
            vm((inner, d), BF16),
            vm((d, RANK), F32),
            vm((2 * RANK, d), BF16),
            vm((2 * NX, RANK, rows), BF16),
            vm((RANK, inner), F32),
            vm((inner, d), BF16),
            vm((ndp, pr, pc), BF16),
            vm((ndp, pr, pc), BF16),
            vm((ndp, pr, pc), BF16),
            vm((RANK, inner), BF16),
            vm((2, RANK // 2, 2 * RANK), F32),
            vm((NX, RANK // 2, 2 * RANK), F32),
            vm((RANK, 2 * RANK), F32),
            vm((RANK, d), F32),
            vm((nplane, zr, zc), F32),
            vm((nplane, zr, zc), F32),
            vm((nz, zr, zc), F32),
            vm((nplane, zr, zc), F32),
            vm((inner, 3 * RANK), BF16),
            vm((3 * RANK, d), BF16),
            vm((tokens, inner), BF16),
            vm((inner, d), BF16),
            vm((d, RANK), F32),
            dma((BLOCKS + 4,)),
            dma((9,)),
            dma, dma, dma,
            dma((BLOCKS,)), dma((BLOCKS,)), dma((BLOCKS,)), dma((BLOCKS,)), dma((BLOCKS,)),
            dma((2,)), dma((2,)), dma((2,)), dma((2,)), dma((3,)), dma((3,)),
        ],
        compiler_params=pltpu.CompilerParams(
            collective_id=0, has_side_effects=True, vmem_limit_bytes=56 * 2**20
        ),
    )(context, out_grad, out_weight, error, q_init)


def solution(mesh):
    ndp = mesh.shape["dp"]
    ny = 4 if ndp % 4 == 0 else 1
    placed = (
        P("dp", "tensor"),
        P(("dp", "tensor"), None),
        P("tensor", None),
        P("dp", "tensor", None),
        P(),
    )
    return jax.shard_map(
        functools.partial(shards, ny, ndp // ny),
        mesh=mesh,
        in_specs=placed,
        out_specs=(P("dp", "tensor"), P("dp", "tensor", None), P()),
        check_vma=False,
    )
```

time: 508 us -> 74.9 us (0.15)
  waiting for transfers between devices: 418 us -> 0 us
  Pallas kernels: 0 us -> 64.1 us
  matrix products: 37 us -> 0 us
  blocking collectives: 24.7 us -> 0 us
  between operations: 13.8 us -> 0.64 us
  other arithmetic: 13 us -> 0 us
  local copies, waits for them, and re-layouts: 1.41 us -> 9.99 us
    psum x2 -> x0, waiting for transfers between devices: 376 us -> none  [the longest x1 239 us: shards(): q_factor = lax.psum(q_part, ('dp', 'tensor')) / replicas]
    pallas_call x0 -> x1, Pallas kernels: none -> 64.1 us  [shards(): pl.pallas_call(functools.partial(kernel, ny, nz), out_shape=(jax.ShapeDty...]
    all_gather x1 -> x0, waiting for transfers between devices: 40.8 us -> none  [shards(): piece = lax.all_gather(out_grad, 'tensor', axis=0, tiled=True)]
    dot_general x6 -> x0, matrix products: 35.6 us -> none  [the longest x1 8.31 us: shards(): lax.dot_general(piece, out_weight, (((1,), (1,)), ((), ())), preferred_el...]
    psum x1 -> x0, blocking collectives: 24.7 us -> none  [shards(): gram = lax.psum(jnp.dot(p_mean.T, p_mean, precision=HIGH), 'tensor')]
    another operation x5 -> x0, other arithmetic: 12.1 us -> none  [the longest x3 6.52 us: shards(): chol = jnp.linalg.cholesky(gram)]
    unnamed x10 -> x5, local copies, waits for them, and re-layouts: 1.34 us -> 8.06 us
  transfers between devices with their start and end apart: 3 -> 0, of which waited for: 3 -> 0; matrix products, arithmetic and copies ran while one was open for 2% -> 0% of each run, Pallas kernels for 0% -> 0%
where the time goes in v1:
time: 74.9 us; the launch traced here: 74.7 us
  Pallas kernels  64.1 us (86%)
  local copies, waits for them, and re-layouts  9.99 us (13%)
    pallas_call x1, Pallas kernels, shards(): pl.pallas_call(functools.partial(kernel, ny, nz), out_shape=(jax.ShapeDty...  64.1 us
    unnamed x5, local copies, waits for them, and re-layouts  8.06 us
    pallas_call x1, local copies, waits for them, and re-layouts, shards(): pl.pallas_call(functools.partial(kernel, ny, nz), out_shape=(jax.ShapeDty...  1.93 us

profile of v1, /device:TPU:1, one launch (start us, length us, event | category | flops | bytes accessed | tf_op | source)
XLA Modules:
  0.0 74.7 jit_solution(12827097653354988995)
XLA Ops:
  0.6 1.9 %copy.8.q_hbm = f32[1024,64]{1,0:T(8,128)} copy(f32[1024,64]{0,1:T(8,128)} %param.9) | data formatting | bytes 524288 | tf_op args[4]
  2.6 64.1 %shard_map.76 = (bf16[2048,1024]{1,0:T(8,128)(2,1)}, bf16[1,1024,1024]{2,1,0:T(8,128)(2,1)}, f32[1024,64]{1,0:T(8,128)}) custom-call(bf16[2048,1024]{1,0:T(8,128)(2,1)} %ctx_hbm.1, bf16[256,1024]{1,0:T(8,128)(2,1)} %dy_hbm.1, bf16[1024,1024]{1,0:T(8,128)(2,1)} %w_hbm.1, bf16[1,1024,1024]{2,1,0:T(8,128)(2,1)} %e_hbm.1, f32[1024,64]{1,0:T(8,128)} %copy.8.q_hbm), custom_call_target="tpu_custom_call" | custom-call | tf_op jit(solution)/shard_map/pallas_call | solution.py:333
  66.7 1.9 %copy.9 = f32[1024,64]{0,1:T(8,128)} copy(f32[1024,64]{1,0:T(8,128)} %get-tuple-element.5) | data formatting | bytes 524288 | tf_op jit(solution)/shard_map/pallas_call | solution.py:333
  68.6 0.0 copy-start
  68.6 4.8 %copy.12 = bf16[2048,1024]{1,0:T(8,128)(2,1)} copy(bf16[2048,1024]{1,0:T(8,128)(2,1)} %get-tuple-element.9) | data formatting | bytes 8388608
  73.4 0.0 copy-done
  73.4 1.3 %copy.13 = bf16[1,1024,1024]{2,1,0:T(8,128)(2,1)} copy(bf16[1,1024,1024]{2,1,0:T(8,128)(2,1)S(1)} %copy-done) | data formatting | bytes 4194304
Async XLA Ops:
  68.6 4.8 %copy-start = (bf16[1,1024,1024]{2,1,0:T(8,128)(2,1)S(1)}, bf16[1,1024,1024]{2,1,0:T(8,128)(2,1)}, u32[]{:S(2)}) copy-start(bf16[1,1024,1024]{2,1,0:T(8,128)(2,1)} %get-tuple-element.10) | copy-start | bytes 6291460

commit v2 on v1

--- a/solution.py
+++ b/solution.py
@@ -28,20 +28,27 @@
 
 def eliminate(a, first, last):
     row_ids = lax.broadcasted_iota(jnp.int32, a.shape, 0)
-    for k in range(first, last):
-        col = jnp.broadcast_to(a[:, k : k + 1], a.shape)
-        row = a[k : k + 1, :] / col[k : k + 1, :]
-        a = a - jnp.where(row_ids > k, col, 0.0) * row
+    for k in range(first, last, 2):
+        c0 = jnp.broadcast_to(a[:, k : k + 1], a.shape)
+        c1 = jnp.broadcast_to(a[:, k + 1 : k + 2], a.shape)
+        r0, r1 = a[k : k + 1, :], a[k + 1 : k + 2, :]
+        aa, bb, cc = c0[k : k + 1, :], c0[k + 1 : k + 2, :], c1[k + 1 : k + 2, :]
+        inv = 1.0 / (aa * cc - bb * bb)
+        w0 = (cc * r0 - bb * r1) * inv
+        w1 = (aa * r1 - bb * r0) * inv
+        second = r1 - (bb / aa) * r0
+        below = a - c0 * w0 - c1 * w1
+        a = jnp.where(row_ids > k + 1, below, jnp.where(row_ids == k + 1, second, a))
     return a
 
 
 def kernel(
     ny, nz,
     ctx_hbm, dy_hbm, w_hbm, e_hbm, q_hbm,
-    dctx_hbm, ne_hbm, qf_hbm,
-    cv, ct, og, wv, ev, qv, q2, yg, pe, gb, ps, prx, pall, pt,
-    gx1, gx2, aug, ze, zs, z1, z2, zall, ft, qs, cs, ns, qo,
-    load, store, y_send, y_near, y_sib, o_send, o_left, o_right, o_far, o_sib,
+    cs, gb, ev, ft, lf, zq,
+    cv, ct, og, wv, qv, q2, yg, pe, ps, prx, pall, pt,
+    gx1, gx2, aug, ze, zs, z1, z2, zall,
+    load, y_send, y_near, y_sib, o_send, o_left, o_right, o_far, o_sib,
     p_send, p_recv, g_send, g_recv, z_send, z_recv,
 ):
     dp, ten = lax.axis_index("dp"), lax.axis_index("tensor")
@@ -62,11 +69,11 @@
 
     @pl.loop(1, nten)
     def _(j):
-        pl.semaphore_signal(barrier, inc=1, device_id={"tensor": lax.rem(ten + j, nten)}, device_id_type=MESH)
+        pl.semaphore_signal(barrier, inc=1, device_id={"tensor": jnp.where(ten + j >= nten, ten + j - nten, ten + j)}, device_id_type=MESH)
 
     @pl.loop(1, ndp)
     def _(j):
-        pl.semaphore_signal(barrier, inc=1, device_id={"dp": lax.rem(dp + j, ndp)}, device_id_type=MESH)
+        pl.semaphore_signal(barrier, inc=1, device_id={"dp": jnp.where(dp + j >= ndp, dp + j - ndp, dp + j)}, device_id_type=MESH)
 
     def piece(b, owner, part=None):
         if part is None:
@@ -77,6 +84,33 @@
         pltpu.make_async_remote_copy(
             src_ref=src, dst_ref=dst, send_sem=s_sem, recv_sem=r_sem, device_id=dev, device_id_type=MESH
         ).start()
+
+    def wrap(i, n):
+        return jnp.where(i >= n, i - n, i)
+
+    def each_replica(act):
+        for j in range(1, ny):
+            to_y = wrap(y + j, ny)
+            act(z * ny + to_y, {"dp": z * ny + to_y})
+
+        @pl.loop(1, nz)
+        def _(i):
+            to_z = wrap(z + i, nz)
+            for j in range(ny):
+                to = to_z * ny + wrap(y + j, ny)
+                act(to, {"dp": to})
+
+    def each_in_plane(act):
+        for j in range(1, ny):
+            to_y = wrap(y + j, ny)
+            act(ten * ny + to_y, {"dp": z * ny + to_y})
+
+        @pl.loop(1, nten)
+        def _(i):
+            to_t = wrap(ten + i, nten)
+            for j in range(ny):
+                to_y = wrap(y + j, ny)
+                act(to_t * ny + to_y, {"dp": z * ny + to_y, "tensor": to_t})
 
     def await_bytes(ref, sem):
         pltpu.make_async_copy(ref, ref, sem).wait()
@@ -92,7 +126,7 @@
         c.start()
 
     load_q.wait()
-    hi, lo = split(qv[...].T)
+    hi, lo = split(qv[...])
     q2[0:RANK] = hi
     q2[RANK : 2 * RANK] = lo
     for c in loads:
@@ -166,10 +200,7 @@
     for k in range(ndp):
         ps[k] = pv[(k % ny) * pr : (k % ny + 1) * pr, (k // ny) * pc : (k // ny + 1) * pc]
 
-    @pl.loop(1, ndp)
-    def _(j):
-        to = lax.rem(dp + j, ndp)
-        send(ps.at[to], prx.at[dp], p_send.at[0], p_recv.at[0], {"dp": to})
+    each_replica(lambda to, dev: send(ps.at[to], prx.at[dp], p_send.at[0], p_recv.at[0], dev))
 
     prx[dp] = ps[dp]
     pass_near(0)
@@ -181,9 +212,7 @@
         total += prx[k].astype(F32)
     pall[dp] = (total * (1.0 / ndp)).astype(BF16)
 
-    @pl.loop(1, ndp)
-    def _(j):
-        send(pall.at[dp], pall.at[dp], p_send.at[1], p_recv.at[1], {"dp": lax.rem(dp + j, ndp)})
+    each_replica(lambda to, dev: send(pall.at[dp], pall.at[dp], p_send.at[1], p_recv.at[1], dev))
 
     pass_near(1)
     send_own(3)
@@ -210,25 +239,22 @@
     await_bytes(gx2.at[pl.ds(0, NX - 1)], g_recv.at[1])
     gram = gx2[0] + gx2[1] + gx2[2] + gx2[3]
     gram = jnp.concatenate([gram[:, :RANK], gram[:, RANK:]], axis=0)
-    eye = (
-        lax.broadcasted_iota(jnp.int32, (RANK, RANK), 0) == lax.broadcasted_iota(jnp.int32, (RANK, RANK), 1)
-    ).astype(F32)
-    aug[...] = eliminate(jnp.concatenate([gram, eye], axis=1), 0, 24)
+    on_diag = lax.broadcasted_iota(jnp.int32, (RANK, RANK), 0) == lax.broadcasted_iota(jnp.int32, (RANK, RANK), 1)
+    diag = jnp.where(on_diag, gram, 0.0)
+    scale = 1.0 / jnp.sqrt(jnp.sum(diag, axis=1, keepdims=True))
+    across = 1.0 / jnp.sqrt(jnp.sum(diag, axis=0, keepdims=True))
+    gram = jnp.where(on_diag, 1.0, gram * scale * across)
+    aug[...] = eliminate(jnp.concatenate([gram, jnp.where(on_diag, across, 0.0)], axis=1), 0, RANK // 2)
     grad_block(2)
     pass_far(3)
     grad_block(3)
 
-    zv = ze[...] + dot(pt[...], gb[...])
+    zv = (ze[...] + dot(pt[...], gb[...])).astype(BF16)
     zr, zc = RANK // ny, d // nten
     for k in range(nplane):
         zs[k] = zv[(k % ny) * zr : (k % ny + 1) * zr, (k // ny) * zc : (k // ny + 1) * zc]
     me = ten * ny + y
-
-    @pl.loop(1, nplane)
-    def _(j):
-        to = lax.rem(me + j, nplane)
-        send(zs.at[to], z1.at[me], z_send.at[0], z_recv.at[0], {"dp": z * ny + to % ny, "tensor": to // ny})
-
+    each_in_plane(lambda to, dev: send(zs.at[to], z1.at[me], z_send.at[0], z_recv.at[0], dev))
     z1[me] = zs[me]
 
     load_w.wait()
@@ -242,69 +268,46 @@
             for b in range(1, BLOCKS):
                 acc += dot(og[b, r, :], wv[c, b * width : (b + 1) * width], NT)
             cs[r, c] = acc.astype(BF16)
-        out = pltpu.make_async_copy(cs.at[r], dctx_hbm.at[r], store.at[i])
-        out.start()
-        return out
-
-    outs = [ctx_chunk(0), ctx_chunk(1)]
+
+    ctx_chunk(0)
+    ctx_chunk(1)
 
     await_bytes(z1.at[pl.ds(0, nplane - 1)], z_recv.at[0])
-    total = z1[0]
+    total = z1[0].astype(F32)
     for k in range(1, nplane):
-        total += z1[k]
+        total += z1[k].astype(F32)
     z2[z] = total
 
     @pl.loop(1, nz)
-    def _(j):
-        to = lax.rem(z + j, nz)
-        send(z2.at[z], z2.at[z], z_send.at[1], z_recv.at[1], {"dp": to * ny + y})
-
-    a = eliminate(aug[...], 24, RANK)
-    on_diag = lax.broadcasted_iota(jnp.int32, (RANK, RANK), 0) == lax.broadcasted_iota(jnp.int32, (RANK, RANK), 1)
+    def _(i):
+        to = wrap(z + i, nz) * ny + y
+        send(z2.at[z], z2.at[z], z_send.at[1], z_recv.at[1], {"dp": to})
+
+    a = eliminate(aug[...], RANK // 2, RANK)
     diag = jnp.sum(jnp.where(on_diag, a[:, :RANK], 0.0), axis=1, keepdims=True)
     inv = a[:, RANK:] / jnp.sqrt(diag)
     inv_hi, inv_lo = split(inv)
-    f = dot(inv_hi, pt[...]) + dot(inv_lo, pt[...])
-    f_hi, f_lo = split(f)
-    ft[...] = jnp.concatenate([f_hi, f_lo, f_hi], axis=0).T
+    lf[...] = jnp.concatenate([inv_hi, inv_lo], axis=1)
 
     await_bytes(z2.at[pl.ds(0, nz - 1)], z_recv.at[1])
     total = z2[0]
     for k in range(1, nz):
         total += z2[k]
-    zall[me] = total * (1.0 / ndp)
-
-    @pl.loop(1, nplane)
-    def _(j):
-        to = lax.rem(me + j, nplane)
-        send(zall.at[me], zall.at[me], z_send.at[2], z_recv.at[2], {"dp": z * ny + to % ny, "tensor": to // ny})
-
-    outs += [ctx_chunk(2), ctx_chunk(3)]
+    zall[me] = (total * (1.0 / ndp)).astype(BF16)
+    each_in_plane(lambda to, dev: send(zall.at[me], zall.at[me], z_send.at[2], z_recv.at[2], dev))
+
+    f = dot(inv_hi, pt[...]) + dot(inv_lo, pt[...])
+    f_hi, f_lo = split(f)
+    up_hi, up_lo = split(inv.T)
+    pg_hi, pg_lo = split(dot(up_hi, f_hi) + dot(up_hi, f_lo) + dot(up_lo, f_hi))
+    ft[...] = jnp.concatenate([pg_hi, pg_lo], axis=0).T
+
+    ctx_chunk(2)
+    ctx_chunk(3)
 
     await_bytes(zall.at[pl.ds(0, nplane - 1)], z_recv.at[2])
     for k in range(nplane):
-        hi, lo = split(zall[k])
-        r, c = (k % ny) * zr, slice((k // ny) * zc, (k // ny + 1) * zc)
-        qs[r : r + zr, c] = hi
-        qs[RANK + r : RANK + r + zr, c] = hi
-        qs[2 * RANK + r : 2 * RANK + r + zr, c] = lo
-    qt = dot(jnp.concatenate([inv_hi, inv_lo, inv_hi], axis=1), qs[...])
-    qo[...] = qt.T
-    out = pltpu.make_async_copy(qo, qf_hbm, store.at[4])
-    out.start()
-    outs.append(out)
-    hi, lo = split(qt)
-    qs[0:RANK] = hi
-    qs[RANK : 2 * RANK] = hi
-    qs[2 * RANK : 3 * RANK] = lo
-    ne_rows = inner // 4
-    for i in range(4):
-        r = pl.ds(i * ne_rows, ne_rows)
-        low = dot(ft[r, :], qs[...])
-        ns[r, :] = (gb[r, :].astype(F32) + ev[r, :].astype(F32) - low).astype(BF16)
-        out = pltpu.make_async_copy(ns.at[r], ne_hbm.at[0, r], store.at[5 + i])
-        out.start()
-        outs.append(out)
+        zq[(k % ny) * zr : (k % ny + 1) * zr, (k // ny) * zc : (k // ny + 1) * zc] = zall[k]
 
     await_bytes(yg.at[pl.ds(0, 7)], y_send)
     for b in range(BLOCKS):
@@ -316,6 +319,27 @@
     await_bytes(z1.at[pl.ds(0, nplane - 1)], z_send.at[0])
     await_bytes(z2.at[pl.ds(0, nz - 1)], z_send.at[1])
     await_bytes(zall.at[pl.ds(0, nplane - 1)], z_send.at[2])
+
+
+def finish(cs, gb, ev, ft, lf, zq, dctx_hbm, ne_hbm, qf_hbm, ns, qo, store):
+    outs = []
+
+    def put(src, dst):
+        out = pltpu.make_async_copy(src, dst, store.at[len(outs)])
+        out.start()
+        outs.append(out)
+
+    put(cs, dctx_hbm)
+    zz = jnp.concatenate([zq[...], zq[...]], axis=0)
+    step = ns.shape[0] // 4
+    for i in range(4):
+        r = pl.ds(i * step, step)
+        low = dot(ft[r, :], zz)
+        ns[r, :] = (gb[r, :].astype(F32) + ev[r, :].astype(F32) - low).astype(BF16)
+        put(ns.at[r], ne_hbm.at[0, r])
+        if i == 0:
+            qo[...] = dot(lf[...], zz)
+            put(qo, qf_hbm)
     for out in outs:
         out.wait()
 
@@ -326,30 +350,31 @@
     ndp, nplane = ny * nz, 2 * NX * ny
     width = d // BLOCKS
     dma = pltpu.SemaphoreType.DMA
-    any_ = pl.BlockSpec(memory_space=pl.ANY)
+    hbm, in_vmem = pl.BlockSpec(memory_space=pltpu.HBM), pl.BlockSpec(memory_space=pltpu.VMEM)
     pr, pc = RANK // ny, inner // nz
     zr, zc = RANK // ny, d // (2 * NX)
     vm = pltpu.VMEM
-    return pl.pallas_call(
+    kept = pl.pallas_call(
         functools.partial(kernel, ny, nz),
         out_shape=(
-            jax.ShapeDtypeStruct((tokens, inner), BF16),
-            jax.ShapeDtypeStruct((1, inner, d), BF16),
-            jax.ShapeDtypeStruct((d, RANK), F32),
+            vm((tokens, inner), BF16),
+            vm((inner, d), BF16),
+            vm((inner, d), BF16),
+            vm((inner, 2 * RANK), BF16),
+            vm((RANK, 2 * RANK), BF16),
+            vm((RANK, d), BF16),
         ),
-        in_specs=[any_] * 5,
-        out_specs=(any_, any_, any_),
+        in_specs=[hbm] * 5,
+        out_specs=(in_vmem,) * 6,
         scratch_shapes=[
             vm((tokens, inner), BF16),
             vm((inner, tokens), BF16),
             vm((BLOCKS, tokens, width), BF16),
             vm((inner, d), BF16),
-            vm((inner, d), BF16),
-            vm((d, RANK), F32),
+            vm((RANK, d), F32),
             vm((2 * RANK, d), BF16),
             vm((2 * NX, RANK, rows), BF16),
             vm((RANK, inner), F32),
-            vm((inner, d), BF16),
             vm((ndp, pr, pc), BF16),
             vm((ndp, pr, pc), BF16),
             vm((ndp, pr, pc), BF16),
@@ -358,25 +383,32 @@
             vm((NX, RANK // 2, 2 * RANK), F32),
             vm((RANK, 2 * RANK), F32),
             vm((RANK, d), F32),
-            vm((nplane, zr, zc), F32),
-            vm((nplane, zr, zc), F32),
+            vm((nplane, zr, zc), BF16),
+            vm((nplane, zr, zc), BF16),
             vm((nz, zr, zc), F32),
-            vm((nplane, zr, zc), F32),
-            vm((inner, 3 * RANK), BF16),
-            vm((3 * RANK, d), BF16),
-            vm((tokens, inner), BF16),
-            vm((inner, d), BF16),
-            vm((d, RANK), F32),
+            vm((nplane, zr, zc), BF16),
             dma((BLOCKS + 4,)),
-            dma((9,)),
             dma, dma, dma,
             dma((BLOCKS,)), dma((BLOCKS,)), dma((BLOCKS,)), dma((BLOCKS,)), dma((BLOCKS,)),
             dma((2,)), dma((2,)), dma((2,)), dma((2,)), dma((3,)), dma((3,)),
         ],
         compiler_params=pltpu.CompilerParams(
-            collective_id=0, has_side_effects=True, vmem_limit_bytes=56 * 2**20
+            collective_id=0, has_side_effects=True, vmem_limit_bytes=40 * 2**20
         ),
-    )(context, out_grad, out_weight, error, q_init)
+    )(*(pltpu.with_memory_space_constraint(v, pltpu.HBM) for v in (context, out_grad, out_weight, error, q_init.T)))
+    dctx, ne, qf = pl.pallas_call(
+        finish,
+        out_shape=(
+            jax.ShapeDtypeStruct((tokens, inner), BF16),
+            jax.ShapeDtypeStruct((1, inner, d), BF16),
+            jax.ShapeDtypeStruct((RANK, d), F32),
+        ),
+        in_specs=[in_vmem] * 6,
+        out_specs=(hbm,) * 3,
+        scratch_shapes=[vm((inner, d), BF16), vm((RANK, d), F32), dma((6,))],
+        compiler_params=pltpu.CompilerParams(vmem_limit_bytes=12 * 2**20),
+    )(*kept)
+    return dctx, ne, qf.T
 
 
 def solution(mesh):

time: 74.9 us -> 61.1 us (0.82)
  local copies, waits for them, and re-layouts: 9.99 us -> 0 us
  Pallas kernels: 64.1 us -> 60.3 us
    unnamed x5 -> x0, local copies, waits for them, and re-layouts: 8.06 us -> none
    pallas_call x1 -> x2, Pallas kernels: 64.1 us -> 60.3 us  [the longest x1 57.6 us: shards(): pl.pallas_call(functools.partial(kernel, ny, nz), out_shape=(vm((tokens,...]
    pallas_call x1 -> x0, local copies, waits for them, and re-layouts: 1.93 us -> none  [shards(): pl.pallas_call(functools.partial(kernel, ny, nz), out_shape=(jax.ShapeDty...]
where the time goes in v2:
time: 61.1 us; the launch traced here: 61 us
  Pallas kernels  60.3 us (99%)
  between operations  0.64 us (1%)
    pallas_call x1, Pallas kernels, shards(): pl.pallas_call(functools.partial(kernel, ny, nz), out_shape=(vm((tokens,...  57.6 us
    pallas_call x1, Pallas kernels, shards(): pl.pallas_call(finish, out_shape=(jax.ShapeDtypeStruct((tokens, inner), B...  2.78 us

profile of v2, /device:TPU:1, one launch (start us, length us, event | category | flops | bytes accessed | tf_op | source)
XLA Modules:
  0.0 61.0 jit_solution(4554129638807420690)
XLA Ops:
  0.6 57.6 %shard_map.76 = (bf16[2048,1024]{1,0:T(8,128)(2,1)S(1)}, bf16[1024,1024]{1,0:T(8,128)(2,1)S(1)}, bf16[1024,1024]{1,0:T(8,128)(2,1)S(1)}, bf16[1024,128]{1,0:T(8,...) custom-call(bf16[2048,1024]{1,0:T(8,128)(2,1)} %ctx_hbm.1, bf16[256,1024]{1,0:T(8,128)(2,1)} %dy_hbm.1, ...), custom_call_target="tpu_custom_call" | custom-call | tf_op jit(solution)/shard_map/pallas_call | solution.py:357
  58.2 2.8 %shard_map.77 = (bf16[2048,1024]{1,0:T(8,128)(2,1)}, bf16[1,1024,1024]{2,1,0:T(8,128)(2,1)}, f32[64,1024]{1,0:T(8,128)}) custom-call(bf16[2048,1024]{1,0:T(8,128)(2,1)S(1)} %get-tuple-element.12.cs, bf16[1024,1024]{1,0:T(8,128)(2,1)S(1)} %get-tuple-element.13.gb, bf16[1024,1024]{1,0:T(8,128)(2,1)S(1)} %get-tuple-element.14.ev, ...), custom_call_target="tpu_custom_call" | custom-call | tf_op jit(solution)/shard_map/pallas_call | solution.py:399

commit v3 on v2

--- a/solution.py
+++ b/solution.py
@@ -12,7 +12,7 @@
 BF16 = jnp.bfloat16
 NX = 4
 RANK = 64
-BLOCKS = 4
+FIRST = 16
 NT = (((1,), (1,)), ((), ()))
 NN = (((1,), (0,)), ((), ()))
 
@@ -46,7 +46,7 @@
     ny, nz,
     ctx_hbm, dy_hbm, w_hbm, e_hbm, q_hbm,
     cs, gb, ev, ft, lf, zq,
-    cv, ct, og, wv, qv, q2, yg, pe, ps, prx, pall, pt,
+    cv, ct, og, wv, wt, acc, qv, q2, yg, pe, ps, prx, pall, pt,
     gx1, gx2, aug, ze, zs, z1, z2, zall,
     load, y_send, y_near, y_sib, o_send, o_left, o_right, o_far, o_sib,
     p_send, p_recv, g_send, g_recv, z_send, z_recv,
@@ -59,7 +59,6 @@
     rows = dy_hbm.shape[0]
     half = rows // 2
     tokens = rows * nten
-    width = og.shape[2]
     inner, d = w_hbm.shape
     xl, xr, xo = lax.rem(x + NX - 1, NX), lax.rem(x + 1, NX), lax.rem(x + 2, NX)
     sib = {"tensor": 2 * x + 1 - core}
@@ -75,10 +74,10 @@
     def _(j):
         pl.semaphore_signal(barrier, inc=1, device_id={"dp": jnp.where(dp + j >= ndp, dp + j - ndp, dp + j)}, device_id_type=MESH)
 
-    def piece(b, owner, part=None):
+    def piece(owner, part=None):
         if part is None:
-            return og.at[b, pl.ds(pl.multiple_of(owner * rows, rows), rows)]
-        return og.at[b, pl.ds(pl.multiple_of(owner * rows + part * half, half), half)]
+            return og.at[pl.ds(pl.multiple_of(owner * rows, rows), rows)]
+        return og.at[pl.ds(pl.multiple_of(owner * rows + part * half, half), half)]
 
     def send(src, dst, s_sem, r_sem, dev):
         pltpu.make_async_remote_copy(
@@ -115,26 +114,21 @@
     def await_bytes(ref, sem):
         pltpu.make_async_copy(ref, ref, sem).wait()
 
-    loads = []
-    for b in range(BLOCKS):
-        loads.append(pltpu.make_async_copy(dy_hbm.at[:, pl.ds(b * width, width)], piece(b, ten), load.at[b]))
-    load_q = pltpu.make_async_copy(q_hbm, qv, load.at[BLOCKS])
-    load_e = pltpu.make_async_copy(e_hbm.at[0], ev, load.at[BLOCKS + 1])
-    load_c = pltpu.make_async_copy(ctx_hbm, cv, load.at[BLOCKS + 2])
-    load_w = pltpu.make_async_copy(w_hbm, wv, load.at[BLOCKS + 3])
-    for c in [load_q, *loads, load_e, load_c, load_w]:
+    mine = piece(ten)
+    load_dy = pltpu.make_async_copy(dy_hbm, mine, load.at[0])
+    load_q = pltpu.make_async_copy(q_hbm, qv, load.at[1])
+    load_e = pltpu.make_async_copy(e_hbm.at[0], ev, load.at[2])
+    load_c = pltpu.make_async_copy(ctx_hbm, cv, load.at[3])
+    load_w = pltpu.make_async_copy(w_hbm, wv, load.at[4])
+    for c in (load_q, load_dy, load_e, load_c, load_w):
         c.start()
 
     load_q.wait()
     hi, lo = split(qv[...])
     q2[0:RANK] = hi
     q2[RANK : 2 * RANK] = lo
-    for c in loads:
-        c.wait()
-    yv = jnp.zeros((2 * RANK, rows), F32)
-    own = pl.ds(pl.multiple_of(ten * rows, rows), rows)
-    for b in range(BLOCKS):
-        yv += dot(q2[:, b * width : (b + 1) * width], og[b, own, :], NT)
+    load_dy.wait()
+    yv = dot(q2[...], mine[...], NT)
     yg[ten] = (yv[:RANK] + yv[RANK:]).astype(BF16)
 
     pl.semaphore_wait(barrier, nten - 1 + ndp - 1)
@@ -143,45 +137,41 @@
         send(yg.at[ten], yg.at[ten], y_send, y_near, dev)
     send(yg.at[ten], yg.at[ten], y_send, y_sib, sib)
 
-    def send_own(b):
-        mine = piece(b, ten)
-        send(mine, mine, o_send.at[b], o_left.at[b], right)
-        send(mine, mine, o_send.at[b], o_right.at[b], left)
-        send(mine, mine, o_send.at[b], o_sib.at[b], sib)
-
-    def pass_near(b):
-        from_left, from_right = piece(b, 2 * xl + core), piece(b, 2 * xr + core)
-        await_bytes(from_left, o_left.at[b])
-        onward = piece(b, 2 * xl + core, 0)
-        send(onward, onward, o_send.at[b], o_far.at[b], right)
-        send(from_left, from_left, o_send.at[b], o_sib.at[b], sib)
-        await_bytes(from_right, o_right.at[b])
-        onward = piece(b, 2 * xr + core, 1)
-        send(onward, onward, o_send.at[b], o_far.at[b], left)
-        send(from_right, from_right, o_send.at[b], o_sib.at[b], sib)
-
-    def pass_far(b):
-        from_far = piece(b, 2 * xo + core)
-        await_bytes(from_far, o_far.at[b])
-        send(from_far, from_far, o_send.at[b], o_sib.at[b], sib)
-
-    def grad_block(b):
-        await_bytes(og.at[b, pl.ds(0, rows * NX)], o_sib.at[b])
-        mt = min(512, inner)
-
-        @pl.loop(0, inner // mt)
-        def _(i):
-            r = pl.ds(pl.multiple_of(i * mt, mt), mt)
-            gb[r, b * width : (b + 1) * width] = dot(ct[r, :], og[b]).astype(BF16)
-
-    send_own(0)
-    send_own(1)
+    def pass_on(ref, sem, dev):
+        send(ref, ref, o_send, sem, dev)
+
+    for first in (0, 1):
+        pass_on(piece(ten, first), o_left.at[first], right)
+        pass_on(piece(ten, 1 - first), o_right.at[1 - first], left)
+    pass_on(mine, o_sib.at[0], sib)
+
+    def arrive(owner, part, sem):
+        await_bytes(piece(owner, part), sem)
+
+    from_left, from_right, from_far = 2 * xl + core, 2 * xr + core, 2 * xo + core
+
+    def rows_of(chip):
+        return pl.ds(pl.multiple_of(2 * chip * rows, 2 * rows), 2 * rows)
+
+    mt = inner // 2
+
+    def grad_rows(k, first=False, last=False):
+        for i in range(2):
+            r = slice(i * mt, (i + 1) * mt)
+            v = dot(ct[r, k], og[k, :])
+            if not first:
+                v += acc[r, :]
+            if last:
+                gb[r, :] = v.astype(BF16)
+            else:
+                acc[r, :] = v
+
+    def ctx_rows(k):
+        cs[k, :] = dot(og[k, :], wt[...]).astype(BF16)
 
     load_e.wait()
-    for n in range(4):
-        r = slice(n * inner // 4, (n + 1) * inner // 4)
-        v = dot(q2[...], ev[r, :], NT)
-        pe[:, r] = v[:RANK] + v[RANK:]
+    v = dot(q2[...], ev[...], NT)
+    pe[...] = v[:RANK] + v[RANK:]
     load_c.wait()
     for t in range(nten):
         ct[:, t * rows : (t + 1) * rows] = cv[t * rows : (t + 1) * rows, :].T
@@ -190,11 +180,11 @@
     for i in (xl, xr, xo):
         got = yg.at[2 * i + core]
         send(got, got, y_send, y_sib, sib)
+    load_w.wait()
+    wt[...] = wv[...].T
     await_bytes(yg.at[pl.ds(0, 4)], y_sib)
 
-    pv = pe[...]
-    for t in range(nten):
-        pv += dot(yg[t], cv[t * rows : (t + 1) * rows, :])
+    pv = pe[...] + dot(jnp.concatenate([yg[t] for t in range(nten)], axis=1), cv[...])
     pr, pc = RANK // ny, inner // nz
     pv = pv.astype(BF16)
     for k in range(ndp):
@@ -203,21 +193,26 @@
     each_replica(lambda to, dev: send(ps.at[to], prx.at[dp], p_send.at[0], p_recv.at[0], dev))
 
     prx[dp] = ps[dp]
-    pass_near(0)
-    send_own(2)
+
+    await_bytes(mine, o_sib.at[0])
+    grad_rows(rows_of(x), first=True)
+    arrive(from_left, 0, o_left.at[0])
+    pass_on(piece(from_left, 0), o_far.at[0], right)
+    arrive(from_right, 1, o_right.at[1])
+    pass_on(piece(from_right, 1), o_far.at[1], left)
 
     await_bytes(prx.at[pl.ds(0, ndp - 1)], p_recv.at[0])
     total = prx[0].astype(F32)
     for k in range(1, ndp):
         total += prx[k].astype(F32)
     pall[dp] = (total * (1.0 / ndp)).astype(BF16)
-
     each_replica(lambda to, dev: send(pall.at[dp], pall.at[dp], p_send.at[1], p_recv.at[1], dev))
 
-    pass_near(1)
-    send_own(3)
-    pass_far(0)
-    grad_block(0)
+    ctx_rows(rows_of(x))
+    arrive(from_left, 1, o_left.at[1])
+    pass_on(piece(from_left), o_sib.at[1], sib)
+    arrive(from_right, 0, o_right.at[0])
+    pass_on(piece(from_right), o_sib.at[2], sib)
 
     await_bytes(pall.at[pl.ds(0, ndp - 1)], p_recv.at[1])
     for k in range(ndp):
@@ -225,16 +220,15 @@
     gram = dot(pt[...], pt[...], NT)
     gx1[core] = jnp.concatenate([gram[: RANK // 2], gram[RANK // 2 :]], axis=1)
     send(gx1.at[core], gx1.at[core], g_send.at[0], g_recv.at[0], sib)
-    pass_far(1)
-    pass_near(2)
     ze[...] = dot(pt[...], ev[...])
     await_bytes(gx1.at[0], g_recv.at[0])
     gx2[x] = gx1[0] + gx1[1]
     for dev in (right, left, far):
         send(gx2.at[x], gx2.at[x], g_send.at[1], g_recv.at[1], dev)
-    grad_block(1)
-    pass_near(3)
-    pass_far(2)
+    await_bytes(piece(from_left), o_sib.at[1])
+    grad_rows(rows_of(xl))
+    await_bytes(piece(from_right), o_sib.at[2])
+    grad_rows(rows_of(xr))
 
     await_bytes(gx2.at[pl.ds(0, NX - 1)], g_recv.at[1])
     gram = gx2[0] + gx2[1] + gx2[2] + gx2[3]
@@ -244,10 +238,15 @@
     scale = 1.0 / jnp.sqrt(jnp.sum(diag, axis=1, keepdims=True))
     across = 1.0 / jnp.sqrt(jnp.sum(diag, axis=0, keepdims=True))
     gram = jnp.where(on_diag, 1.0, gram * scale * across)
-    aug[...] = eliminate(jnp.concatenate([gram, jnp.where(on_diag, across, 0.0)], axis=1), 0, RANK // 2)
-    grad_block(2)
-    pass_far(3)
-    grad_block(3)
+    aug[...] = eliminate(jnp.concatenate([gram, jnp.where(on_diag, across, 0.0)], axis=1), 0, FIRST)
+    for part in (0, 1):
+        arrive(from_far, part, o_far.at[part])
+        pass_on(piece(from_far, part), o_sib.at[3 + part], sib)
+    grad_rows(pl.ds(pl.multiple_of(from_far * rows, rows), rows))
+    for part in (0, 1):
+        arrive(from_far, part, o_sib.at[3 + part])
+    other = 2 * xo + 1 - core
+    grad_rows(pl.ds(pl.multiple_of(other * rows, rows), rows), last=True)
 
     zv = (ze[...] + dot(pt[...], gb[...])).astype(BF16)
     zr, zc = RANK // ny, d // nten
@@ -257,20 +256,8 @@
     each_in_plane(lambda to, dev: send(zs.at[to], z1.at[me], z_send.at[0], z_recv.at[0], dev))
     z1[me] = zs[me]
 
-    load_w.wait()
-    out_rows = tokens // 4
-
-    def ctx_chunk(i):
-        r = pl.ds(i * out_rows, out_rows)
-        for n in range(4):
-            c = slice(n * inner // 4, (n + 1) * inner // 4)
-            acc = dot(og[0, r, :], wv[c, 0:width], NT)
-            for b in range(1, BLOCKS):
-                acc += dot(og[b, r, :], wv[c, b * width : (b + 1) * width], NT)
-            cs[r, c] = acc.astype(BF16)
-
-    ctx_chunk(0)
-    ctx_chunk(1)
+    ctx_rows(rows_of(xl))
+    ctx_rows(rows_of(xr))
 
     await_bytes(z1.at[pl.ds(0, nplane - 1)], z_recv.at[0])
     total = z1[0].astype(F32)
@@ -283,7 +270,7 @@
         to = wrap(z + i, nz) * ny + y
         send(z2.at[z], z2.at[z], z_send.at[1], z_recv.at[1], {"dp": to})
 
-    a = eliminate(aug[...], RANK // 2, RANK)
+    a = eliminate(aug[...], FIRST, RANK)
     diag = jnp.sum(jnp.where(on_diag, a[:, :RANK], 0.0), axis=1, keepdims=True)
     inv = a[:, RANK:] / jnp.sqrt(diag)
     inv_hi, inv_lo = split(inv)
@@ -302,16 +289,14 @@
     pg_hi, pg_lo = split(dot(up_hi, f_hi) + dot(up_hi, f_lo) + dot(up_lo, f_hi))
     ft[...] = jnp.concatenate([pg_hi, pg_lo], axis=0).T
 
-    ctx_chunk(2)
-    ctx_chunk(3)
+    ctx_rows(rows_of(xo))
 
     await_bytes(zall.at[pl.ds(0, nplane - 1)], z_recv.at[2])
     for k in range(nplane):
         zq[(k % ny) * zr : (k % ny + 1) * zr, (k // ny) * zc : (k // ny + 1) * zc] = zall[k]
 
     await_bytes(yg.at[pl.ds(0, 7)], y_send)
-    for b in range(BLOCKS):
-        await_bytes(og.at[b, pl.ds(0, 7 * rows)], o_send.at[b])
+    await_bytes(og.at[pl.ds(0, 7 * rows)], o_send)
     await_bytes(prx.at[pl.ds(0, ndp - 1)], p_send.at[0])
     await_bytes(pall.at[pl.ds(0, ndp - 1)], p_send.at[1])
     await_bytes(gx1.at[0], g_send.at[0])
@@ -348,7 +333,6 @@
     tokens, inner = context.shape
     rows, d = out_grad.shape
     ndp, nplane = ny * nz, 2 * NX * ny
-    width = d // BLOCKS
     dma = pltpu.SemaphoreType.DMA
     hbm, in_vmem = pl.BlockSpec(memory_space=pltpu.HBM), pl.BlockSpec(memory_space=pltpu.VMEM)
     pr, pc = RANK // ny, inner // nz
@@ -369,8 +353,10 @@
         scratch_shapes=[
             vm((tokens, inner), BF16),
             vm((inner, tokens), BF16),
-            vm((BLOCKS, tokens, width), BF16),
+            vm((tokens, d), BF16),
             vm((inner, d), BF16),
+            vm((d, inner), BF16),
+            vm((inner, d), F32),
             vm((RANK, d), F32),
             vm((2 * RANK, d), BF16),
             vm((2 * NX, RANK, rows), BF16),
@@ -387,9 +373,9 @@
             vm((nplane, zr, zc), BF16),
             vm((nz, zr, zc), F32),
             vm((nplane, zr, zc), BF16),
-            dma((BLOCKS + 4,)),
+            dma((5,)),
             dma, dma, dma,
-            dma((BLOCKS,)), dma((BLOCKS,)), dma((BLOCKS,)), dma((BLOCKS,)), dma((BLOCKS,)),
+            dma, dma((2,)), dma((2,)), dma((2,)), dma((5,)),
             dma((2,)), dma((2,)), dma((2,)), dma((2,)), dma((3,)), dma((3,)),
         ],
         compiler_params=pltpu.CompilerParams(

time: 61.1 us -> 59.5 us (0.974)
  Pallas kernels: 60.3 us -> 58.8 us
    pallas_call x1, Pallas kernels: 57.6 us -> 56 us  [shards(): pl.pallas_call(functools.partial(kernel, ny, nz), out_shape=(vm((tokens,...]
where the time goes in v3:
time: 59.5 us; the launch traced here: 59.4 us
  Pallas kernels  58.8 us (99%)
  between operations  0.64 us (1%)
    pallas_call x1, Pallas kernels, shards(): pl.pallas_call(functools.partial(kernel, ny, nz), out_shape=(vm((tokens,...  56 us
    pallas_call x1, Pallas kernels, shards(): pl.pallas_call(finish, out_shape=(jax.ShapeDtypeStruct((tokens, inner), B...  2.78 us

profile of v3, /device:TPU:1, one launch (start us, length us, event | category | flops | bytes accessed | tf_op | source)
XLA Modules:
  0.0 59.4 jit_solution(7458432550549485429)
XLA Ops:
  0.6 56.0 %shard_map.76 = (bf16[2048,1024]{1,0:T(8,128)(2,1)S(1)}, bf16[1024,1024]{1,0:T(8,128)(2,1)S(1)}, bf16[1024,1024]{1,0:T(8,128)(2,1)S(1)}, bf16[1024,128]{1,0:T(8,...) custom-call(bf16[2048,1024]{1,0:T(8,128)(2,1)} %ctx_hbm.1, bf16[256,1024]{1,0:T(8,128)(2,1)} %dy_hbm.1, ...), custom_call_target="tpu_custom_call" | custom-call | tf_op jit(solution)/shard_map/pallas_call | solution.py:341
  56.6 2.8 %shard_map.77 = (bf16[2048,1024]{1,0:T(8,128)(2,1)}, bf16[1,1024,1024]{2,1,0:T(8,128)(2,1)}, f32[64,1024]{1,0:T(8,128)}) custom-call(bf16[2048,1024]{1,0:T(8,128)(2,1)S(1)} %get-tuple-element.12.cs, bf16[1024,1024]{1,0:T(8,128)(2,1)S(1)} %get-tuple-element.13.gb, bf16[1024,1024]{1,0:T(8,128)(2,1)S(1)} %get-tuple-element.14.ev, ...), custom_call_target="tpu_custom_call" | custom-call | tf_op jit(solution)/shard_map/pallas_call | solution.py:385

commit v4 on v3

--- a/solution.py
+++ b/solution.py
@@ -12,7 +12,6 @@
 BF16 = jnp.bfloat16
 NX = 4
 RANK = 64
-FIRST = 16
 NT = (((1,), (1,)), ((), ()))
 NN = (((1,), (0,)), ((), ()))
 
@@ -26,9 +25,9 @@
     return hi, (v - hi.astype(F32)).astype(BF16)
 
 
-def eliminate(a, first, last):
+def eliminate(a):
     row_ids = lax.broadcasted_iota(jnp.int32, a.shape, 0)
-    for k in range(first, last, 2):
+    for k in range(0, a.shape[0], 2):
         c0 = jnp.broadcast_to(a[:, k : k + 1], a.shape)
         c1 = jnp.broadcast_to(a[:, k + 1 : k + 2], a.shape)
         r0, r1 = a[k : k + 1, :], a[k + 1 : k + 2, :]
@@ -47,7 +46,7 @@
     ctx_hbm, dy_hbm, w_hbm, e_hbm, q_hbm,
     cs, gb, ev, ft, lf, zq,
     cv, ct, og, wv, wt, acc, qv, q2, yg, pe, ps, prx, pall, pt,
-    gx1, gx2, aug, ze, zs, z1, z2, zall,
+    gx1, gx2, ze, zs, z1, z2, zall,
     load, y_send, y_near, y_sib, o_send, o_left, o_right, o_far, o_sib,
     p_send, p_recv, g_send, g_recv, z_send, z_recv,
 ):
@@ -64,16 +63,6 @@
     sib = {"tensor": 2 * x + 1 - core}
     left, right, far = ({"tensor": 2 * i + core} for i in (xl, xr, xo))
 
-    barrier = pltpu.get_barrier_semaphore()
-
-    @pl.loop(1, nten)
-    def _(j):
-        pl.semaphore_signal(barrier, inc=1, device_id={"tensor": jnp.where(ten + j >= nten, ten + j - nten, ten + j)}, device_id_type=MESH)
-
-    @pl.loop(1, ndp)
-    def _(j):
-        pl.semaphore_signal(barrier, inc=1, device_id={"dp": jnp.where(dp + j >= ndp, dp + j - ndp, dp + j)}, device_id_type=MESH)
-
     def piece(owner, part=None):
         if part is None:
             return og.at[pl.ds(pl.multiple_of(owner * rows, rows), rows)]
@@ -87,29 +76,37 @@
     def wrap(i, n):
         return jnp.where(i >= n, i - n, i)
 
+    def far_first(n, act):
+        act(n // 2)
+
+        @pl.loop(0, n // 2 - 1)
+        def _(i):
+            act(n // 2 - 1 - i)
+            act(n // 2 + 1 + i)
+
     def each_replica(act):
-        for j in range(1, ny):
-            to_y = wrap(y + j, ny)
-            act(z * ny + to_y, {"dp": z * ny + to_y})
-
-        @pl.loop(1, nz)
-        def _(i):
+        def at_z(i):
             to_z = wrap(z + i, nz)
             for j in range(ny):
                 to = to_z * ny + wrap(y + j, ny)
                 act(to, {"dp": to})
 
-    def each_in_plane(act):
+        far_first(nz, at_z)
         for j in range(1, ny):
             to_y = wrap(y + j, ny)
-            act(ten * ny + to_y, {"dp": z * ny + to_y})
-
-        @pl.loop(1, nten)
-        def _(i):
+            act(z * ny + to_y, {"dp": z * ny + to_y})
+
+    def each_in_plane(act):
+        def at_tensor(i):
             to_t = wrap(ten + i, nten)
             for j in range(ny):
                 to_y = wrap(y + j, ny)
                 act(to_t * ny + to_y, {"dp": z * ny + to_y, "tensor": to_t})
+
+        far_first(nten, at_tensor)
+        for j in range(1, ny):
+            to_y = wrap(y + j, ny)
+            act(ten * ny + to_y, {"dp": z * ny + to_y})
 
     def await_bytes(ref, sem):
         pltpu.make_async_copy(ref, ref, sem).wait()
@@ -120,7 +117,20 @@
     load_e = pltpu.make_async_copy(e_hbm.at[0], ev, load.at[2])
     load_c = pltpu.make_async_copy(ctx_hbm, cv, load.at[3])
     load_w = pltpu.make_async_copy(w_hbm, wv, load.at[4])
-    for c in (load_q, load_dy, load_e, load_c, load_w):
+    load_q.start()
+    load_dy.start()
+
+    barrier = pltpu.get_barrier_semaphore()
+
+    @pl.loop(1, nten)
+    def _(j):
+        pl.semaphore_signal(barrier, inc=1, device_id={"tensor": jnp.where(ten + j >= nten, ten + j - nten, ten + j)}, device_id_type=MESH)
+
+    @pl.loop(1, ndp)
+    def _(j):
+        pl.semaphore_signal(barrier, inc=1, device_id={"dp": jnp.where(dp + j >= ndp, dp + j - ndp, dp + j)}, device_id_type=MESH)
+
+    for c in (load_e, load_c, load_w):
         c.start()
 
     load_q.wait()
@@ -133,7 +143,7 @@
 
     pl.semaphore_wait(barrier, nten - 1 + ndp - 1)
 
-    for dev in (right, left, far):
+    for dev in (far, right, left):
         send(yg.at[ten], yg.at[ten], y_send, y_near, dev)
     send(yg.at[ten], yg.at[ten], y_send, y_sib, sib)
 
@@ -172,16 +182,17 @@
     load_e.wait()
     v = dot(q2[...], ev[...], NT)
     pe[...] = v[:RANK] + v[RANK:]
-    load_c.wait()
-    for t in range(nten):
-        ct[:, t * rows : (t + 1) * rows] = cv[t * rows : (t + 1) * rows, :].T
-
     await_bytes(yg.at[pl.ds(0, 3)], y_near)
     for i in (xl, xr, xo):
         got = yg.at[2 * i + core]
         send(got, got, y_send, y_sib, sib)
-    load_w.wait()
-    wt[...] = wv[...].T
+    load_c.wait()
+
+    def turn(t):
+        ct[:, t * rows : (t + 1) * rows] = cv[t * rows : (t + 1) * rows, :].T
+
+    for t in range(nten // 2):
+        turn(t)
     await_bytes(yg.at[pl.ds(0, 4)], y_sib)
 
     pv = pe[...] + dot(jnp.concatenate([yg[t] for t in range(nten)], axis=1), cv[...])
@@ -194,6 +205,8 @@
 
     prx[dp] = ps[dp]
 
+    for t in range(nten // 2, nten):
+        turn(t)
     await_bytes(mine, o_sib.at[0])
     grad_rows(rows_of(x), first=True)
     arrive(from_left, 0, o_left.at[0])
@@ -208,11 +221,21 @@
     pall[dp] = (total * (1.0 / ndp)).astype(BF16)
     each_replica(lambda to, dev: send(pall.at[dp], pall.at[dp], p_send.at[1], p_recv.at[1], dev))
 
-    ctx_rows(rows_of(x))
+    load_w.wait()
+    wt[...] = wv[...].T
     arrive(from_left, 1, o_left.at[1])
     pass_on(piece(from_left), o_sib.at[1], sib)
     arrive(from_right, 0, o_right.at[0])
     pass_on(piece(from_right), o_sib.at[2], sib)
+    ctx_rows(rows_of(x))
+    await_bytes(piece(from_left), o_sib.at[1])
+    grad_rows(rows_of(xl))
+    await_bytes(piece(from_right), o_sib.at[2])
+    grad_rows(rows_of(xr))
+    for part in (0, 1):
+        arrive(from_far, part, o_far.at[part])
+        pass_on(piece(from_far, part), o_sib.at[3 + part], sib)
+    grad_rows(pl.ds(pl.multiple_of(from_far * rows, rows), rows))
 
     await_bytes(pall.at[pl.ds(0, ndp - 1)], p_recv.at[1])
     for k in range(ndp):
@@ -221,14 +244,33 @@
     gx1[core] = jnp.concatenate([gram[: RANK // 2], gram[RANK // 2 :]], axis=1)
     send(gx1.at[core], gx1.at[core], g_send.at[0], g_recv.at[0], sib)
     ze[...] = dot(pt[...], ev[...])
+    for part in (0, 1):
+        arrive(from_far, part, o_sib.at[3 + part])
+    other = 2 * xo + 1 - core
+    grad_rows(pl.ds(pl.multiple_of(other * rows, rows), rows), last=True)
+
+    zv = (ze[...] + dot(pt[...], gb[...])).astype(BF16)
+    zr, zc = RANK // ny, d // nten
+    for k in range(nplane):
+        zs[k] = zv[(k % ny) * zr : (k % ny + 1) * zr, (k // ny) * zc : (k // ny + 1) * zc]
+    me = ten * ny + y
+    each_in_plane(lambda to, dev: send(zs.at[to], z1.at[me], z_send.at[0], z_recv.at[0], dev))
+    z1[me] = zs[me]
+
     await_bytes(gx1.at[0], g_recv.at[0])
     gx2[x] = gx1[0] + gx1[1]
-    for dev in (right, left, far):
+    for dev in (far, right, left):
         send(gx2.at[x], gx2.at[x], g_send.at[1], g_recv.at[1], dev)
-    await_bytes(piece(from_left), o_sib.at[1])
-    grad_rows(rows_of(xl))
-    await_bytes(piece(from_right), o_sib.at[2])
-    grad_rows(rows_of(xr))
+    ctx_rows(rows_of(xl))
+    ctx_rows(rows_of(xr))
+
+    await_bytes(z1.at[pl.ds(0, nplane - 1)], z_recv.at[0])
+    total = z1[0].astype(F32)
+    for k in range(1, nplane):
+        total += z1[k].astype(F32)
+    z2[z] = total
+
+    far_first(nz, lambda i: send(z2.at[z], z2.at[z], z_send.at[1], z_recv.at[1], {"dp": wrap(z + i, nz) * ny + y}))
 
     await_bytes(gx2.at[pl.ds(0, NX - 1)], g_recv.at[1])
     gram = gx2[0] + gx2[1] + gx2[2] + gx2[3]
@@ -238,39 +280,7 @@
     scale = 1.0 / jnp.sqrt(jnp.sum(diag, axis=1, keepdims=True))
     across = 1.0 / jnp.sqrt(jnp.sum(diag, axis=0, keepdims=True))
     gram = jnp.where(on_diag, 1.0, gram * scale * across)
-    aug[...] = eliminate(jnp.concatenate([gram, jnp.where(on_diag, across, 0.0)], axis=1), 0, FIRST)
-    for part in (0, 1):
-        arrive(from_far, part, o_far.at[part])
-        pass_on(piece(from_far, part), o_sib.at[3 + part], sib)
-    grad_rows(pl.ds(pl.multiple_of(from_far * rows, rows), rows))
-    for part in (0, 1):
-        arrive(from_far, part, o_sib.at[3 + part])
-    other = 2 * xo + 1 - core
-    grad_rows(pl.ds(pl.multiple_of(other * rows, rows), rows), last=True)
-
-    zv = (ze[...] + dot(pt[...], gb[...])).astype(BF16)
-    zr, zc = RANK // ny, d // nten
-    for k in range(nplane):
-        zs[k] = zv[(k % ny) * zr : (k % ny + 1) * zr, (k // ny) * zc : (k // ny + 1) * zc]
-    me = ten * ny + y
-    each_in_plane(lambda to, dev: send(zs.at[to], z1.at[me], z_send.at[0], z_recv.at[0], dev))
-    z1[me] = zs[me]
-
-    ctx_rows(rows_of(xl))
-    ctx_rows(rows_of(xr))
-
-    await_bytes(z1.at[pl.ds(0, nplane - 1)], z_recv.at[0])
-    total = z1[0].astype(F32)
-    for k in range(1, nplane):
-        total += z1[k].astype(F32)
-    z2[z] = total
-
-    @pl.loop(1, nz)
-    def _(i):
-        to = wrap(z + i, nz) * ny + y
-        send(z2.at[z], z2.at[z], z_send.at[1], z_recv.at[1], {"dp": to})
-
-    a = eliminate(aug[...], FIRST, RANK)
+    a = eliminate(jnp.concatenate([gram, jnp.where(on_diag, across, 0.0)], axis=1))
     diag = jnp.sum(jnp.where(on_diag, a[:, :RANK], 0.0), axis=1, keepdims=True)
     inv = a[:, RANK:] / jnp.sqrt(diag)
     inv_hi, inv_lo = split(inv)
@@ -367,7 +377,6 @@
             vm((RANK, inner), BF16),
             vm((2, RANK // 2, 2 * RANK), F32),
             vm((NX, RANK // 2, 2 * RANK), F32),
-            vm((RANK, 2 * RANK), F32),
             vm((RANK, d), F32),
             vm((nplane, zr, zc), BF16),
             vm((nplane, zr, zc), BF16),

time: 59.5 us -> 53.2 us (0.89)
  Pallas kernels: 58.8 us -> 52.4 us
    pallas_call x1, Pallas kernels: 56 us -> 49.7 us  [shards(): pl.pallas_call(functools.partial(kernel, ny, nz), out_shape=(vm((tokens,...]
where the time goes in v4:
time: 53.2 us; the launch traced here: 53.1 us
  Pallas kernels  52.4 us (98%)
  between operations  0.64 us (1%)
    pallas_call x1, Pallas kernels, shards(): pl.pallas_call(functools.partial(kernel, ny, nz), out_shape=(vm((tokens,...  49.7 us
    pallas_call x1, Pallas kernels, shards(): pl.pallas_call(finish, out_shape=(jax.ShapeDtypeStruct((tokens, inner), B...  2.78 us

profile of v4, /device:TPU:1, one launch (start us, length us, event | category | flops | bytes accessed | tf_op | source)
XLA Modules:
  0.0 53.1 jit_solution(15756695092564898099)
XLA Ops:
  0.6 49.7 %shard_map.76 = (bf16[2048,1024]{1,0:T(8,128)(2,1)S(1)}, bf16[1024,1024]{1,0:T(8,128)(2,1)S(1)}, bf16[1024,1024]{1,0:T(8,128)(2,1)S(1)}, bf16[1024,128]{1,0:T(8,...) custom-call(bf16[2048,1024]{1,0:T(8,128)(2,1)} %ctx_hbm.1, bf16[256,1024]{1,0:T(8,128)(2,1)} %dy_hbm.1, ...), custom_call_target="tpu_custom_call" | custom-call | tf_op jit(solution)/shard_map/pallas_call | solution.py:351
  50.3 2.8 %shard_map.77 = (bf16[2048,1024]{1,0:T(8,128)(2,1)}, bf16[1,1024,1024]{2,1,0:T(8,128)(2,1)}, f32[64,1024]{1,0:T(8,128)}) custom-call(bf16[2048,1024]{1,0:T(8,128)(2,1)S(1)} %get-tuple-element.12.cs, bf16[1024,1024]{1,0:T(8,128)(2,1)S(1)} %get-tuple-element.13.gb, bf16[1024,1024]{1,0:T(8,128)(2,1)S(1)} %get-tuple-element.14.ev, ...), custom_call_target="tpu_custom_call" | custom-call | tf_op jit(solution)/shard_map/pallas_call | solution.py:394

commit v5 on v4

--- a/solution.py
+++ b/solution.py
@@ -46,7 +46,7 @@
     ctx_hbm, dy_hbm, w_hbm, e_hbm, q_hbm,
     cs, gb, ev, ft, lf, zq,
     cv, ct, og, wv, wt, acc, qv, q2, yg, pe, ps, prx, pall, pt,
-    gx1, gx2, ze, zs, z1, z2, zall,
+    gx1, gx2, zs, z1, z2, zall,
     load, y_send, y_near, y_sib, o_send, o_left, o_right, o_far, o_sib,
     p_send, p_recv, g_send, g_recv, z_send, z_recv,
 ):
@@ -63,10 +63,13 @@
     sib = {"tensor": 2 * x + 1 - core}
     left, right, far = ({"tensor": 2 * i + core} for i in (xl, xr, xo))
 
-    def piece(owner, part=None):
+    OWN, LEFT, RIGHT, FAR = 0, 1, 2, 3
+
+    def piece(slot, part=None, of=core):
+        start = 2 * slot * rows + of * rows
         if part is None:
-            return og.at[pl.ds(pl.multiple_of(owner * rows, rows), rows)]
-        return og.at[pl.ds(pl.multiple_of(owner * rows + part * half, half), half)]
+            return og.at[pl.ds(pl.multiple_of(start, rows), rows)]
+        return og.at[pl.ds(pl.multiple_of(start + part * half, half), half)]
 
     def send(src, dst, s_sem, r_sem, dev):
         pltpu.make_async_remote_copy(
@@ -111,7 +114,7 @@
     def await_bytes(ref, sem):
         pltpu.make_async_copy(ref, ref, sem).wait()
 
-    mine = piece(ten)
+    mine = piece(OWN)
     load_dy = pltpu.make_async_copy(dy_hbm, mine, load.at[0])
     load_q = pltpu.make_async_copy(q_hbm, qv, load.at[1])
     load_e = pltpu.make_async_copy(e_hbm.at[0], ev, load.at[2])
@@ -147,37 +150,27 @@
         send(yg.at[ten], yg.at[ten], y_send, y_near, dev)
     send(yg.at[ten], yg.at[ten], y_send, y_sib, sib)
 
-    def pass_on(ref, sem, dev):
-        send(ref, ref, o_send, sem, dev)
+    def pass_on(src, dst, sem, dev):
+        send(src, dst, o_send, sem, dev)
 
     for first in (0, 1):
-        pass_on(piece(ten, first), o_left.at[first], right)
-        pass_on(piece(ten, 1 - first), o_right.at[1 - first], left)
-    pass_on(mine, o_sib.at[0], sib)
-
-    def arrive(owner, part, sem):
-        await_bytes(piece(owner, part), sem)
-
-    from_left, from_right, from_far = 2 * xl + core, 2 * xr + core, 2 * xo + core
-
-    def rows_of(chip):
-        return pl.ds(pl.multiple_of(2 * chip * rows, 2 * rows), 2 * rows)
+        pass_on(piece(OWN, first), piece(LEFT, first), o_left.at[first], right)
+        pass_on(piece(OWN, 1 - first), piece(RIGHT, 1 - first), o_right.at[1 - first], left)
+    pass_on(mine, mine, o_sib.at[0], sib)
+
+    def hand_over(slot, part, sem):
+        ref = piece(slot, part)
+        pass_on(ref, ref, sem, sib)
+
+    def slots(first, count=1):
+        return slice(2 * first * rows, 2 * (first + count) * rows)
 
     mt = inner // 2
-
-    def grad_rows(k, first=False, last=False):
-        for i in range(2):
-            r = slice(i * mt, (i + 1) * mt)
-            v = dot(ct[r, k], og[k, :])
-            if not first:
-                v += acc[r, :]
-            if last:
-                gb[r, :] = v.astype(BF16)
-            else:
-                acc[r, :] = v
-
-    def ctx_rows(k):
-        cs[k, :] = dot(og[k, :], wt[...]).astype(BF16)
+    halves = [slice(i * mt, (i + 1) * mt) for i in range(2)]
+
+    def ctx_rows(slot, chip):
+        to = pl.ds(pl.multiple_of(2 * chip * rows, 2 * rows), 2 * rows)
+        cs[to, :] = dot(og[slots(slot), :], wt[...]).astype(BF16)
 
     load_e.wait()
     v = dot(q2[...], ev[...], NT)
@@ -188,11 +181,13 @@
         send(got, got, y_send, y_sib, sib)
     load_c.wait()
 
-    def turn(t):
-        ct[:, t * rows : (t + 1) * rows] = cv[t * rows : (t + 1) * rows, :].T
-
-    for t in range(nten // 2):
-        turn(t)
+    def turn(slot, chip):
+        for i in range(2):
+            src = pl.ds(pl.multiple_of((2 * chip + i) * rows, rows), rows)
+            ct[:, (2 * slot + i) * rows : (2 * slot + i + 1) * rows] = cv[src, :].T
+
+    turn(OWN, x)
+    turn(LEFT, xl)
     await_bytes(yg.at[pl.ds(0, 4)], y_sib)
 
     pv = pe[...] + dot(jnp.concatenate([yg[t] for t in range(nten)], axis=1), cv[...])
@@ -205,14 +200,18 @@
 
     prx[dp] = ps[dp]
 
-    for t in range(nten // 2, nten):
-        turn(t)
-    await_bytes(mine, o_sib.at[0])
-    grad_rows(rows_of(x), first=True)
-    arrive(from_left, 0, o_left.at[0])
-    pass_on(piece(from_left, 0), o_far.at[0], right)
-    arrive(from_right, 1, o_right.at[1])
-    pass_on(piece(from_right, 1), o_far.at[1], left)
+    turn(RIGHT, xr)
+    turn(FAR, xo)
+    await_bytes(piece(OWN, of=1 - core), o_sib.at[0])
+    for r in halves:
+        acc[r, :] = dot(ct[r, slots(OWN)], og[slots(OWN), :])
+    await_bytes(piece(LEFT, 0), o_left.at[0])
+    pass_on(piece(LEFT, 0), piece(FAR, 0), o_far.at[0], right)
+    await_bytes(piece(RIGHT, 1), o_right.at[1])
+    pass_on(piece(RIGHT, 1), piece(FAR, 1), o_far.at[1], left)
+    load_w.wait()
+    wt[...] = wv[...].T
+    ctx_rows(OWN, x)
 
     await_bytes(prx.at[pl.ds(0, ndp - 1)], p_recv.at[0])
     total = prx[0].astype(F32)
@@ -221,21 +220,20 @@
     pall[dp] = (total * (1.0 / ndp)).astype(BF16)
     each_replica(lambda to, dev: send(pall.at[dp], pall.at[dp], p_send.at[1], p_recv.at[1], dev))
 
-    load_w.wait()
-    wt[...] = wv[...].T
-    arrive(from_left, 1, o_left.at[1])
-    pass_on(piece(from_left), o_sib.at[1], sib)
-    arrive(from_right, 0, o_right.at[0])
-    pass_on(piece(from_right), o_sib.at[2], sib)
-    ctx_rows(rows_of(x))
-    await_bytes(piece(from_left), o_sib.at[1])
-    grad_rows(rows_of(xl))
-    await_bytes(piece(from_right), o_sib.at[2])
-    grad_rows(rows_of(xr))
+    await_bytes(piece(LEFT, 1), o_left.at[1])
+    hand_over(LEFT, None, o_sib.at[1])
+    await_bytes(piece(RIGHT, 0), o_right.at[0])
+    hand_over(RIGHT, None, o_sib.at[2])
+    await_bytes(piece(LEFT, of=1 - core), o_sib.at[1])
+    await_bytes(piece(RIGHT, of=1 - core), o_sib.at[2])
+    for r in halves:
+        v = acc[r, :] + dot(ct[r, slots(LEFT, 2)], og[slots(LEFT, 2), :])
+        acc[r, :] = v
+        gb[r, :] = v.astype(BF16)
+    ctx_rows(LEFT, xl)
     for part in (0, 1):
-        arrive(from_far, part, o_far.at[part])
-        pass_on(piece(from_far, part), o_sib.at[3 + part], sib)
-    grad_rows(pl.ds(pl.multiple_of(from_far * rows, rows), rows))
+        await_bytes(piece(FAR, part), o_far.at[part])
+        hand_over(FAR, part, o_sib.at[3 + part])
 
     await_bytes(pall.at[pl.ds(0, ndp - 1)], p_recv.at[1])
     for k in range(ndp):
@@ -243,13 +241,12 @@
     gram = dot(pt[...], pt[...], NT)
     gx1[core] = jnp.concatenate([gram[: RANK // 2], gram[RANK // 2 :]], axis=1)
     send(gx1.at[core], gx1.at[core], g_send.at[0], g_recv.at[0], sib)
-    ze[...] = dot(pt[...], ev[...])
+
+    zv = dot(pt[...], ev[...]) + dot(pt[...], gb[...])
+    met = dot(pt[...], ct[:, slots(FAR)]).astype(BF16)
     for part in (0, 1):
-        arrive(from_far, part, o_sib.at[3 + part])
-    other = 2 * xo + 1 - core
-    grad_rows(pl.ds(pl.multiple_of(other * rows, rows), rows), last=True)
-
-    zv = (ze[...] + dot(pt[...], gb[...])).astype(BF16)
+        await_bytes(piece(FAR, part, 1 - core), o_sib.at[3 + part])
+    zv = (zv + dot(met, og[slots(FAR), :])).astype(BF16)
     zr, zc = RANK // ny, d // nten
     for k in range(nplane):
         zs[k] = zv[(k % ny) * zr : (k % ny + 1) * zr, (k // ny) * zc : (k // ny + 1) * zc]
@@ -261,8 +258,9 @@
     gx2[x] = gx1[0] + gx1[1]
     for dev in (far, right, left):
         send(gx2.at[x], gx2.at[x], g_send.at[1], g_recv.at[1], dev)
-    ctx_rows(rows_of(xl))
-    ctx_rows(rows_of(xr))
+    for r in halves:
+        gb[r, :] = (acc[r, :] + dot(ct[r, slots(FAR)], og[slots(FAR), :])).astype(BF16)
+    ctx_rows(RIGHT, xr)
 
     await_bytes(z1.at[pl.ds(0, nplane - 1)], z_recv.at[0])
     total = z1[0].astype(F32)
@@ -299,7 +297,7 @@
     pg_hi, pg_lo = split(dot(up_hi, f_hi) + dot(up_hi, f_lo) + dot(up_lo, f_hi))
     ft[...] = jnp.concatenate([pg_hi, pg_lo], axis=0).T
 
-    ctx_rows(rows_of(xo))
+    ctx_rows(FAR, xo)
 
     await_bytes(zall.at[pl.ds(0, nplane - 1)], z_recv.at[2])
     for k in range(nplane):
@@ -324,7 +322,9 @@
         out.start()
         outs.append(out)
 
-    put(cs, dctx_hbm)
+    part = cs.shape[0] // 4
+    for i in range(4):
+        put(cs.at[pl.ds(i * part, part)], dctx_hbm.at[pl.ds(i * part, part)])
     zz = jnp.concatenate([zq[...], zq[...]], axis=0)
     step = ns.shape[0] // 4
     for i in range(4):
@@ -377,7 +377,6 @@
             vm((RANK, inner), BF16),
             vm((2, RANK // 2, 2 * RANK), F32),
             vm((NX, RANK // 2, 2 * RANK), F32),
-            vm((RANK, d), F32),
             vm((nplane, zr, zc), BF16),
             vm((nplane, zr, zc), BF16),
             vm((nz, zr, zc), F32),
@@ -400,7 +399,7 @@
         ),
         in_specs=[in_vmem] * 6,
         out_specs=(hbm,) * 3,
-        scratch_shapes=[vm((inner, d), BF16), vm((RANK, d), F32), dma((6,))],
+        scratch_shapes=[vm((inner, d), BF16), vm((RANK, d), F32), dma((9,))],
         compiler_params=pltpu.CompilerParams(vmem_limit_bytes=12 * 2**20),
     )(*kept)
     return dctx, ne, qf.T

time: 53.2 us -> 53.3 us (level)
  no operation moved by 1% of the time
where the time goes in v5:
time: 53.3 us; the launch traced here: 53.2 us
  Pallas kernels  52.6 us (99%)
  between operations  0.64 us (1%)
    pallas_call x1, Pallas kernels, shards(): pl.pallas_call(functools.partial(kernel, ny, nz), out_shape=(vm((tokens,...  49.8 us
    pallas_call x1, Pallas kernels, shards(): pl.pallas_call(finish, out_shape=(jax.ShapeDtypeStruct((tokens, inner), B...  2.81 us

profile of v5, /device:TPU:1, one launch (start us, length us, event | category | flops | bytes accessed | tf_op | source)
XLA Modules:
  0.0 53.2 jit_solution(12043965736760629818)
XLA Ops:
  0.6 49.8 %shard_map.76 = (bf16[2048,1024]{1,0:T(8,128)(2,1)S(1)}, bf16[1024,1024]{1,0:T(8,128)(2,1)S(1)}, bf16[1024,1024]{1,0:T(8,128)(2,1)S(1)}, bf16[1024,128]{1,0:T(8,...) custom-call(bf16[2048,1024]{1,0:T(8,128)(2,1)} %ctx_hbm.1, bf16[256,1024]{1,0:T(8,128)(2,1)} %dy_hbm.1, ...), custom_call_target="tpu_custom_call" | custom-call | tf_op jit(solution)/shard_map/pallas_call | solution.py:351
  50.4 2.8 %shard_map.77 = (bf16[2048,1024]{1,0:T(8,128)(2,1)}, bf16[1,1024,1024]{2,1,0:T(8,128)(2,1)}, f32[64,1024]{1,0:T(8,128)}) custom-call(bf16[2048,1024]{1,0:T(8,128)(2,1)S(1)} %get-tuple-element.12.cs, bf16[1024,1024]{1,0:T(8,128)(2,1)S(1)} %get-tuple-element.13.gb, bf16[1024,1024]{1,0:T(8,128)(2,1)S(1)} %get-tuple-element.14.ev, ...), custom_call_target="tpu_custom_call" | custom-call | tf_op jit(solution)/shard_map/pallas_call | solution.py:393

commit v6 on v5

--- a/solution.py
+++ b/solution.py
@@ -25,9 +25,9 @@
     return hi, (v - hi.astype(F32)).astype(BF16)
 
 
-def eliminate(a):
+def eliminate(a, first, last):
     row_ids = lax.broadcasted_iota(jnp.int32, a.shape, 0)
-    for k in range(0, a.shape[0], 2):
+    for k in range(first, last, 2):
         c0 = jnp.broadcast_to(a[:, k : k + 1], a.shape)
         c1 = jnp.broadcast_to(a[:, k + 1 : k + 2], a.shape)
         r0, r1 = a[k : k + 1, :], a[k + 1 : k + 2, :]
@@ -45,7 +45,7 @@
     ny, nz,
     ctx_hbm, dy_hbm, w_hbm, e_hbm, q_hbm,
     cs, gb, ev, ft, lf, zq,
-    cv, ct, og, wv, wt, acc, qv, q2, yg, pe, ps, prx, pall, pt,
+    cv, ct, og, wv, wt, acc, qv, q2, yg, pe, ps, prx, pex, pall, pt,
     gx1, gx2, zs, z1, z2, zall,
     load, y_send, y_near, y_sib, o_send, o_left, o_right, o_far, o_sib,
     p_send, p_recv, g_send, g_recv, z_send, z_recv,
@@ -87,17 +87,15 @@
             act(n // 2 - 1 - i)
             act(n // 2 + 1 + i)
 
-    def each_replica(act):
-        def at_z(i):
-            to_z = wrap(z + i, nz)
-            for j in range(ny):
-                to = to_z * ny + wrap(y + j, ny)
-                act(to, {"dp": to})
-
-        far_first(nz, at_z)
-        for j in range(1, ny):
-            to_y = wrap(y + j, ny)
-            act(z * ny + to_y, {"dp": z * ny + to_y})
+    q = nz // 2
+    steps = sorted(((d if d <= q // 2 else d - q, d) for d in range(q)), key=lambda p: (-abs(p[0]), p[0]))
+
+    def each_near(sign, act):
+        for step, d in steps:
+            to_z = lax.rem(z + sign * step + nz, nz)
+            for j in range(1 if step == 0 else 0, ny):
+                to_y = wrap(y + j, ny)
+                act(d, to_z, to_y, {"dp": to_z * ny + to_y})
 
     def each_in_plane(act):
         def at_tensor(i):
@@ -191,14 +189,17 @@
     await_bytes(yg.at[pl.ds(0, 4)], y_sib)
 
     pv = pe[...] + dot(jnp.concatenate([yg[t] for t in range(nten)], axis=1), cv[...])
-    pr, pc = RANK // ny, inner // nz
+    pr, pc = RANK // ny, inner // q
     pv = pv.astype(BF16)
-    for k in range(ndp):
+    for k in range(ny * q):
         ps[k] = pv[(k % ny) * pr : (k % ny + 1) * pr, (k // ny) * pc : (k // ny + 1) * pc]
 
-    each_replica(lambda to, dev: send(ps.at[to], prx.at[dp], p_send.at[0], p_recv.at[0], dev))
-
-    prx[dp] = ps[dp]
+    def to_owner(d, to_z, to_y, dev):
+        send(ps.at[lax.rem(to_z, q) * ny + to_y], prx.at[d * ny + y], p_send.at[0], p_recv.at[0], dev)
+
+    each_near(1, to_owner)
+    own_piece = lax.rem(z, q) * ny + y
+    prx[y] = ps[own_piece]
 
     turn(RIGHT, xr)
     turn(FAR, xo)
@@ -211,14 +212,20 @@
     pass_on(piece(RIGHT, 1), piece(FAR, 1), o_far.at[1], left)
     load_w.wait()
     wt[...] = wv[...].T
+
+    await_bytes(prx.at[pl.ds(0, ny * q - 1)], p_recv.at[0])
+    total = prx[0].astype(F32)
+    for k in range(1, ny * q):
+        total += prx[k].astype(F32)
+    side = z // q
+    pex[side] = total.astype(BF16)
+    send(pex.at[side], pex.at[side], p_send.at[1], p_recv.at[1], {"dp": lax.rem(z + q, nz) * ny + y})
     ctx_rows(OWN, x)
-
-    await_bytes(prx.at[pl.ds(0, ndp - 1)], p_recv.at[0])
-    total = prx[0].astype(F32)
-    for k in range(1, ndp):
-        total += prx[k].astype(F32)
-    pall[dp] = (total * (1.0 / ndp)).astype(BF16)
-    each_replica(lambda to, dev: send(pall.at[dp], pall.at[dp], p_send.at[1], p_recv.at[1], dev))
+    await_bytes(pex.at[0], p_recv.at[1])
+    pall[own_piece] = ((pex[0].astype(F32) + pex[1].astype(F32)) * (1.0 / ndp)).astype(BF16)
+    each_near(
+        -1, lambda d, to_z, to_y, dev: send(pall.at[own_piece], pall.at[own_piece], p_send.at[2], p_recv.at[2], dev)
+    )
 
     await_bytes(piece(LEFT, 1), o_left.at[1])
     hand_over(LEFT, None, o_sib.at[1])
@@ -235,8 +242,8 @@
         await_bytes(piece(FAR, part), o_far.at[part])
         hand_over(FAR, part, o_sib.at[3 + part])
 
-    await_bytes(pall.at[pl.ds(0, ndp - 1)], p_recv.at[1])
-    for k in range(ndp):
+    await_bytes(pall.at[pl.ds(0, ny * q - 1)], p_recv.at[2])
+    for k in range(ny * q):
         pt[(k % ny) * pr : (k % ny + 1) * pr, (k // ny) * pc : (k // ny + 1) * pc] = pall[k]
     gram = dot(pt[...], pt[...], NT)
     gx1[core] = jnp.concatenate([gram[: RANK // 2], gram[RANK // 2 :]], axis=1)
@@ -262,14 +269,6 @@
         gb[r, :] = (acc[r, :] + dot(ct[r, slots(FAR)], og[slots(FAR), :])).astype(BF16)
     ctx_rows(RIGHT, xr)
 
-    await_bytes(z1.at[pl.ds(0, nplane - 1)], z_recv.at[0])
-    total = z1[0].astype(F32)
-    for k in range(1, nplane):
-        total += z1[k].astype(F32)
-    z2[z] = total
-
-    far_first(nz, lambda i: send(z2.at[z], z2.at[z], z_send.at[1], z_recv.at[1], {"dp": wrap(z + i, nz) * ny + y}))
-
     await_bytes(gx2.at[pl.ds(0, NX - 1)], g_recv.at[1])
     gram = gx2[0] + gx2[1] + gx2[2] + gx2[3]
     gram = jnp.concatenate([gram[:, :RANK], gram[:, RANK:]], axis=0)
@@ -278,16 +277,26 @@
     scale = 1.0 / jnp.sqrt(jnp.sum(diag, axis=1, keepdims=True))
     across = 1.0 / jnp.sqrt(jnp.sum(diag, axis=0, keepdims=True))
     gram = jnp.where(on_diag, 1.0, gram * scale * across)
-    a = eliminate(jnp.concatenate([gram, jnp.where(on_diag, across, 0.0)], axis=1))
+    a = eliminate(jnp.concatenate([gram, jnp.where(on_diag, across, 0.0)], axis=1), 0, RANK // 2)
+
+    await_bytes(z1.at[pl.ds(0, nplane - 1)], z_recv.at[0])
+    total = z1[0].astype(F32)
+    for k in range(1, nplane):
+        total += z1[k].astype(F32)
+    z2[z] = total.astype(BF16)
+
+    far_first(nz, lambda i: send(z2.at[z], z2.at[z], z_send.at[1], z_recv.at[1], {"dp": wrap(z + i, nz) * ny + y}))
+
+    a = eliminate(a, RANK // 2, RANK)
     diag = jnp.sum(jnp.where(on_diag, a[:, :RANK], 0.0), axis=1, keepdims=True)
     inv = a[:, RANK:] / jnp.sqrt(diag)
     inv_hi, inv_lo = split(inv)
     lf[...] = jnp.concatenate([inv_hi, inv_lo], axis=1)
 
     await_bytes(z2.at[pl.ds(0, nz - 1)], z_recv.at[1])
-    total = z2[0]
+    total = z2[0].astype(F32)
     for k in range(1, nz):
-        total += z2[k]
+        total += z2[k].astype(F32)
     zall[me] = (total * (1.0 / ndp)).astype(BF16)
     each_in_plane(lambda to, dev: send(zall.at[me], zall.at[me], z_send.at[2], z_recv.at[2], dev))
 
@@ -305,8 +314,9 @@
 
     await_bytes(yg.at[pl.ds(0, 7)], y_send)
     await_bytes(og.at[pl.ds(0, 7 * rows)], o_send)
-    await_bytes(prx.at[pl.ds(0, ndp - 1)], p_send.at[0])
-    await_bytes(pall.at[pl.ds(0, ndp - 1)], p_send.at[1])
+    await_bytes(prx.at[pl.ds(0, ny * q - 1)], p_send.at[0])
+    await_bytes(pex.at[0], p_send.at[1])
+    await_bytes(pall.at[pl.ds(0, ny * q - 1)], p_send.at[2])
     await_bytes(gx1.at[0], g_send.at[0])
     await_bytes(gx2.at[pl.ds(0, NX - 1)], g_send.at[1])
     await_bytes(z1.at[pl.ds(0, nplane - 1)], z_send.at[0])
@@ -342,10 +352,11 @@
 def shards(ny, nz, context, out_grad, out_weight, error, q_init):
     tokens, inner = context.shape
     rows, d = out_grad.shape
-    ndp, nplane = ny * nz, 2 * NX * ny
+    nplane = 2 * NX * ny
     dma = pltpu.SemaphoreType.DMA
     hbm, in_vmem = pl.BlockSpec(memory_space=pltpu.HBM), pl.BlockSpec(memory_space=pltpu.VMEM)
-    pr, pc = RANK // ny, inner // nz
+    q = nz // 2
+    pr, pc = RANK // ny, inner // q
     zr, zc = RANK // ny, d // (2 * NX)
     vm = pltpu.VMEM
     kept = pl.pallas_call(
@@ -371,20 +382,21 @@
             vm((2 * RANK, d), BF16),
             vm((2 * NX, RANK, rows), BF16),
             vm((RANK, inner), F32),
-            vm((ndp, pr, pc), BF16),
-            vm((ndp, pr, pc), BF16),
-            vm((ndp, pr, pc), BF16),
+            vm((ny * q, pr, pc), BF16),
+            vm((ny * q, pr, pc), BF16),
+            vm((2, pr, pc), BF16),
+            vm((ny * q, pr, pc), BF16),
             vm((RANK, inner), BF16),
             vm((2, RANK // 2, 2 * RANK), F32),
             vm((NX, RANK // 2, 2 * RANK), F32),
             vm((nplane, zr, zc), BF16),
             vm((nplane, zr, zc), BF16),
-            vm((nz, zr, zc), F32),
+            vm((nz, zr, zc), BF16),
             vm((nplane, zr, zc), BF16),
             dma((5,)),
             dma, dma, dma,
             dma, dma((2,)), dma((2,)), dma((2,)), dma((5,)),
-            dma((2,)), dma((2,)), dma((2,)), dma((2,)), dma((3,)), dma((3,)),
+            dma((3,)), dma((3,)), dma((2,)), dma((2,)), dma((3,)), dma((3,)),
         ],
         compiler_params=pltpu.CompilerParams(
             collective_id=0, has_side_effects=True, vmem_limit_bytes=40 * 2**20

time: 53.3 us -> 55.3 us (1.038)
  Pallas kernels: 52.6 us -> 54.5 us
    pallas_call x1, Pallas kernels: 49.8 us -> 51.7 us  [shards(): pl.pallas_call(functools.partial(kernel, ny, nz), out_shape=(vm((tokens,...]
where the time goes in v6:
time: 55.3 us; the launch traced here: 55.2 us
  Pallas kernels  54.5 us (99%)
  between operations  0.64 us (1%)
    pallas_call x1, Pallas kernels, shards(): pl.pallas_call(functools.partial(kernel, ny, nz), out_shape=(vm((tokens,...  51.7 us
    pallas_call x1, Pallas kernels, shards(): pl.pallas_call(finish, out_shape=(jax.ShapeDtypeStruct((tokens, inner), B...  2.81 us

profile of v6, /device:TPU:1, one launch (start us, length us, event | category | flops | bytes accessed | tf_op | source)
XLA Modules:
  0.0 55.2 jit_solution(526223844516916828)
XLA Ops:
  0.6 51.7 %shard_map.76 = (bf16[2048,1024]{1,0:T(8,128)(2,1)S(1)}, bf16[1024,1024]{1,0:T(8,128)(2,1)S(1)}, bf16[1024,1024]{1,0:T(8,128)(2,1)S(1)}, bf16[1024,128]{1,0:T(8,...) custom-call(bf16[2048,1024]{1,0:T(8,128)(2,1)} %ctx_hbm.1, bf16[256,1024]{1,0:T(8,128)(2,1)} %dy_hbm.1, ...), custom_call_target="tpu_custom_call" | custom-call | tf_op jit(solution)/shard_map/pallas_call | solution.py:362
  52.4 2.8 %shard_map.77 = (bf16[2048,1024]{1,0:T(8,128)(2,1)}, bf16[1,1024,1024]{2,1,0:T(8,128)(2,1)}, f32[64,1024]{1,0:T(8,128)}) custom-call(bf16[2048,1024]{1,0:T(8,128)(2,1)S(1)} %get-tuple-element.12.cs, bf16[1024,1024]{1,0:T(8,128)(2,1)S(1)} %get-tuple-element.13.gb, bf16[1024,1024]{1,0:T(8,128)(2,1)S(1)} %get-tuple-element.14.ev, ...), custom_call_target="tpu_custom_call" | custom-call | tf_op jit(solution)/shard_map/pallas_call | solution.py:405

commit v7 on v5

--- a/solution.py
+++ b/solution.py
@@ -202,15 +202,13 @@
 
     turn(RIGHT, xr)
     turn(FAR, xo)
-    await_bytes(piece(OWN, of=1 - core), o_sib.at[0])
-    for r in halves:
-        acc[r, :] = dot(ct[r, slots(OWN)], og[slots(OWN), :])
     await_bytes(piece(LEFT, 0), o_left.at[0])
     pass_on(piece(LEFT, 0), piece(FAR, 0), o_far.at[0], right)
     await_bytes(piece(RIGHT, 1), o_right.at[1])
     pass_on(piece(RIGHT, 1), piece(FAR, 1), o_far.at[1], left)
     load_w.wait()
     wt[...] = wv[...].T
+    await_bytes(piece(OWN, of=1 - core), o_sib.at[0])
     ctx_rows(OWN, x)
 
     await_bytes(prx.at[pl.ds(0, ndp - 1)], p_recv.at[0])
@@ -227,7 +225,7 @@
     await_bytes(piece(LEFT, of=1 - core), o_sib.at[1])
     await_bytes(piece(RIGHT, of=1 - core), o_sib.at[2])
     for r in halves:
-        v = acc[r, :] + dot(ct[r, slots(LEFT, 2)], og[slots(LEFT, 2), :])
+        v = dot(ct[r, slots(OWN, 3)], og[slots(OWN, 3), :])
         acc[r, :] = v
         gb[r, :] = v.astype(BF16)
     ctx_rows(LEFT, xl)
@@ -238,10 +236,6 @@
     await_bytes(pall.at[pl.ds(0, ndp - 1)], p_recv.at[1])
     for k in range(ndp):
         pt[(k % ny) * pr : (k % ny + 1) * pr, (k // ny) * pc : (k // ny + 1) * pc] = pall[k]
-    gram = dot(pt[...], pt[...], NT)
-    gx1[core] = jnp.concatenate([gram[: RANK // 2], gram[RANK // 2 :]], axis=1)
-    send(gx1.at[core], gx1.at[core], g_send.at[0], g_recv.at[0], sib)
-
     zv = dot(pt[...], ev[...]) + dot(pt[...], gb[...])
     met = dot(pt[...], ct[:, slots(FAR)]).astype(BF16)
     for part in (0, 1):
@@ -254,19 +248,25 @@
     each_in_plane(lambda to, dev: send(zs.at[to], z1.at[me], z_send.at[0], z_recv.at[0], dev))
     z1[me] = zs[me]
 
+    gram = dot(pt[...], pt[...], NT)
+    gx1[core] = jnp.concatenate([gram[: RANK // 2], gram[RANK // 2 :]], axis=1)
+    send(gx1.at[core], gx1.at[core], g_send.at[0], g_recv.at[0], sib)
+
+    def last_rows(r):
+        gb[r, :] = (acc[r, :] + dot(ct[r, slots(FAR)], og[slots(FAR), :])).astype(BF16)
+
+    last_rows(halves[0])
     await_bytes(gx1.at[0], g_recv.at[0])
     gx2[x] = gx1[0] + gx1[1]
     for dev in (far, right, left):
         send(gx2.at[x], gx2.at[x], g_send.at[1], g_recv.at[1], dev)
-    for r in halves:
-        gb[r, :] = (acc[r, :] + dot(ct[r, slots(FAR)], og[slots(FAR), :])).astype(BF16)
-    ctx_rows(RIGHT, xr)
+    last_rows(halves[1])
 
     await_bytes(z1.at[pl.ds(0, nplane - 1)], z_recv.at[0])
     total = z1[0].astype(F32)
     for k in range(1, nplane):
         total += z1[k].astype(F32)
-    z2[z] = total
+    z2[z] = total.astype(BF16)
 
     far_first(nz, lambda i: send(z2.at[z], z2.at[z], z_send.at[1], z_recv.at[1], {"dp": wrap(z + i, nz) * ny + y}))
 
@@ -281,13 +281,14 @@
     a = eliminate(jnp.concatenate([gram, jnp.where(on_diag, across, 0.0)], axis=1))
     diag = jnp.sum(jnp.where(on_diag, a[:, :RANK], 0.0), axis=1, keepdims=True)
     inv = a[:, RANK:] / jnp.sqrt(diag)
+    ctx_rows(RIGHT, xr)
     inv_hi, inv_lo = split(inv)
     lf[...] = jnp.concatenate([inv_hi, inv_lo], axis=1)
 
     await_bytes(z2.at[pl.ds(0, nz - 1)], z_recv.at[1])
-    total = z2[0]
+    total = z2[0].astype(F32)
     for k in range(1, nz):
-        total += z2[k]
+        total += z2[k].astype(F32)
     zall[me] = (total * (1.0 / ndp)).astype(BF16)
     each_in_plane(lambda to, dev: send(zall.at[me], zall.at[me], z_send.at[2], z_recv.at[2], dev))
 
@@ -379,7 +380,7 @@
             vm((NX, RANK // 2, 2 * RANK), F32),
             vm((nplane, zr, zc), BF16),
             vm((nplane, zr, zc), BF16),
-            vm((nz, zr, zc), F32),
+            vm((nz, zr, zc), BF16),
             vm((nplane, zr, zc), BF16),
             dma((5,)),
             dma, dma, dma,

time: 53.3 us -> 53.7 us (level)
  no operation moved by 1% of the time
where the time goes in v7:
time: 53.7 us; the launch traced here: 53.6 us
  Pallas kernels  52.9 us (99%)
  between operations  0.64 us (1%)
    pallas_call x1, Pallas kernels, shards(): pl.pallas_call(functools.partial(kernel, ny, nz), out_shape=(vm((tokens,...  50.1 us
    pallas_call x1, Pallas kernels, shards(): pl.pallas_call(finish, out_shape=(jax.ShapeDtypeStruct((tokens, inner), B...  2.81 us

profile of v7, /device:TPU:1, one launch (start us, length us, event | category | flops | bytes accessed | tf_op | source)
XLA Modules:
  0.0 53.6 jit_solution(7868690011524664869)
XLA Ops:
  0.6 50.1 %shard_map.76 = (bf16[2048,1024]{1,0:T(8,128)(2,1)S(1)}, bf16[1024,1024]{1,0:T(8,128)(2,1)S(1)}, bf16[1024,1024]{1,0:T(8,128)(2,1)S(1)}, bf16[1024,128]{1,0:T(8,...) custom-call(bf16[2048,1024]{1,0:T(8,128)(2,1)} %ctx_hbm.1, bf16[256,1024]{1,0:T(8,128)(2,1)} %dy_hbm.1, ...), custom_call_target="tpu_custom_call" | custom-call | tf_op jit(solution)/shard_map/pallas_call | solution.py:352
  50.8 2.8 %shard_map.77 = (bf16[2048,1024]{1,0:T(8,128)(2,1)}, bf16[1,1024,1024]{2,1,0:T(8,128)(2,1)}, f32[64,1024]{1,0:T(8,128)}) custom-call(bf16[2048,1024]{1,0:T(8,128)(2,1)S(1)} %get-tuple-element.12.cs, bf16[1024,1024]{1,0:T(8,128)(2,1)S(1)} %get-tuple-element.13.gb, bf16[1024,1024]{1,0:T(8,128)(2,1)S(1)} %get-tuple-element.14.ev, ...), custom_call_target="tpu_custom_call" | custom-call | tf_op jit(solution)/shard_map/pallas_call | solution.py:394

commit v8 on v7

--- a/solution.py
+++ b/solution.py
@@ -204,8 +204,10 @@
     turn(FAR, xo)
     await_bytes(piece(LEFT, 0), o_left.at[0])
     pass_on(piece(LEFT, 0), piece(FAR, 0), o_far.at[0], right)
+    hand_over(LEFT, 0, o_sib.at[1])
     await_bytes(piece(RIGHT, 1), o_right.at[1])
     pass_on(piece(RIGHT, 1), piece(FAR, 1), o_far.at[1], left)
+    hand_over(RIGHT, 1, o_sib.at[2])
     load_w.wait()
     wt[...] = wv[...].T
     await_bytes(piece(OWN, of=1 - core), o_sib.at[0])
@@ -219,16 +221,17 @@
     each_replica(lambda to, dev: send(pall.at[dp], pall.at[dp], p_send.at[1], p_recv.at[1], dev))
 
     await_bytes(piece(LEFT, 1), o_left.at[1])
-    hand_over(LEFT, None, o_sib.at[1])
+    hand_over(LEFT, 1, o_sib.at[5])
     await_bytes(piece(RIGHT, 0), o_right.at[0])
-    hand_over(RIGHT, None, o_sib.at[2])
-    await_bytes(piece(LEFT, of=1 - core), o_sib.at[1])
-    await_bytes(piece(RIGHT, of=1 - core), o_sib.at[2])
+    hand_over(RIGHT, 0, o_sib.at[6])
+    await_bytes(piece(LEFT, 0, 1 - core), o_sib.at[1])
+    await_bytes(piece(RIGHT, 1, 1 - core), o_sib.at[2])
+    await_bytes(piece(LEFT, 1, 1 - core), o_sib.at[5])
+    await_bytes(piece(RIGHT, 0, 1 - core), o_sib.at[6])
     for r in halves:
         v = dot(ct[r, slots(OWN, 3)], og[slots(OWN, 3), :])
         acc[r, :] = v
         gb[r, :] = v.astype(BF16)
-    ctx_rows(LEFT, xl)
     for part in (0, 1):
         await_bytes(piece(FAR, part), o_far.at[part])
         hand_over(FAR, part, o_sib.at[3 + part])
@@ -261,6 +264,7 @@
     for dev in (far, right, left):
         send(gx2.at[x], gx2.at[x], g_send.at[1], g_recv.at[1], dev)
     last_rows(halves[1])
+    ctx_rows(LEFT, xl)
 
     await_bytes(z1.at[pl.ds(0, nplane - 1)], z_recv.at[0])
     total = z1[0].astype(F32)
@@ -281,7 +285,6 @@
     a = eliminate(jnp.concatenate([gram, jnp.where(on_diag, across, 0.0)], axis=1))
     diag = jnp.sum(jnp.where(on_diag, a[:, :RANK], 0.0), axis=1, keepdims=True)
     inv = a[:, RANK:] / jnp.sqrt(diag)
-    ctx_rows(RIGHT, xr)
     inv_hi, inv_lo = split(inv)
     lf[...] = jnp.concatenate([inv_hi, inv_lo], axis=1)
 
@@ -298,6 +301,7 @@
     pg_hi, pg_lo = split(dot(up_hi, f_hi) + dot(up_hi, f_lo) + dot(up_lo, f_hi))
     ft[...] = jnp.concatenate([pg_hi, pg_lo], axis=0).T
 
+    ctx_rows(RIGHT, xr)
     ctx_rows(FAR, xo)
 
     await_bytes(zall.at[pl.ds(0, nplane - 1)], z_recv.at[2])
@@ -384,7 +388,7 @@
             vm((nplane, zr, zc), BF16),
             dma((5,)),
             dma, dma, dma,
-            dma, dma((2,)), dma((2,)), dma((2,)), dma((5,)),
+            dma, dma((2,)), dma((2,)), dma((2,)), dma((7,)),
             dma((2,)), dma((2,)), dma((2,)), dma((2,)), dma((3,)), dma((3,)),
         ],
         compiler_params=pltpu.CompilerParams(

time: 53.7 us -> 52 us (0.968)
  Pallas kernels: 52.9 us -> 51.1 us
    pallas_call x1, Pallas kernels: 50.1 us -> 48.3 us  [shards(): pl.pallas_call(functools.partial(kernel, ny, nz), out_shape=(vm((tokens,...]
where the time goes in v8:
time: 52 us; the launch traced here: 51.9 us
  Pallas kernels  51.1 us (98%)
  between operations  0.8 us (2%)
    pallas_call x1, Pallas kernels, shards(): pl.pallas_call(functools.partial(kernel, ny, nz), out_shape=(vm((tokens,...  48.3 us
    pallas_call x1, Pallas kernels, shards(): pl.pallas_call(finish, out_shape=(jax.ShapeDtypeStruct((tokens, inner), B...  2.81 us

profile of v8, /device:TPU:1, one launch (start us, length us, event | category | flops | bytes accessed | tf_op | source)
XLA Modules:
  0.0 51.9 jit_solution(5443297559364270337)
XLA Ops:
  0.6 48.3 %shard_map.76 = (bf16[2048,1024]{1,0:T(8,128)(2,1)S(1)}, bf16[1024,1024]{1,0:T(8,128)(2,1)S(1)}, bf16[1024,1024]{1,0:T(8,128)(2,1)S(1)}, bf16[1024,128]{1,0:T(8,...) custom-call(bf16[2048,1024]{1,0:T(8,128)(2,1)} %ctx_hbm.1, bf16[256,1024]{1,0:T(8,128)(2,1)} %dy_hbm.1, ...), custom_call_target="tpu_custom_call" | custom-call | tf_op jit(solution)/shard_map/pallas_call | solution.py:356
  49.0 2.8 %shard_map.77 = (bf16[2048,1024]{1,0:T(8,128)(2,1)}, bf16[1,1024,1024]{2,1,0:T(8,128)(2,1)}, f32[64,1024]{1,0:T(8,128)}) custom-call(bf16[2048,1024]{1,0:T(8,128)(2,1)S(1)} %get-tuple-element.12.cs, bf16[1024,1024]{1,0:T(8,128)(2,1)S(1)} %get-tuple-element.13.gb, bf16[1024,1024]{1,0:T(8,128)(2,1)S(1)} %get-tuple-element.14.ev, ...), custom_call_target="tpu_custom_call" | custom-call | tf_op jit(solution)/shard_map/pallas_call | solution.py:398
